TPU v7x, 256 devices: a whole 4x4x8 slice. The times are simulated.
256 devices in a mesh: chan: 128 (over z_lo, x, y, core), day: 2 (over z_hi).
Axes of the slice: x: 4, y: 4, z: 8 (z_hi: 2, z_lo: 4; z = z_hi * 4 + z_lo), core: 2. Of those that a mesh axis runs over, the one named last changes fastest.
Arguments:
- spectra: bfloat16 [4096, 64, 400], P('chan', 'day'), may hold values from -6 to 6
- owners: int32 [2], replicated, may hold values from 0 to 127
Outputs:
- stacks: bfloat16 [2, 4096, 32, 400], P(None, ('chan', 'day'))
Inputs may be any that keep to these rules, and one draw needn't show every extreme that they name: `owners`: block indices along the channel axis; two steps may name the same block.
All inputs are finite; a program needn't handle non-finite values.
Results may differ from a plain program's by a relative error of at most 0.0073.
Values may be sent and summed in bfloat16 or wider, within the bound.
No kernel may reach another device: no remote copies, remote signals or barrier semaphores. Data moves between devices by JAX's collectives and lax.ppermute only.
A program may use at most 64 MiB of HBM per device.

v0:
```python
import math

import jax
import jax.numpy as jnp
from jax import lax
from jax.sharding import PartitionSpec as P

LAGS = 400
STEPS = 2


def broadcast(array, axis, root):
    mine = lax.axis_index(axis) == root
    return lax.psum(jnp.where(mine, array, jnp.zeros_like(array)), axis)


def whiten(spectra, bins):
    values = spectra.astype(jnp.float32)
    real_part = values[..., :bins]
    imag_part = values[..., bins:]
    power = real_part * real_part + imag_part * imag_part
    mean_power = jnp.mean(power, axis=-1, keepdims=True)
    factor = lax.rsqrt(power + 0.25 * mean_power + 1e-06)
    return jnp.concatenate([real_part * factor, imag_part * factor], axis=-1).astype(jnp.bfloat16)


def lag_table(bins, lag_count):
    freqs = jnp.arange(bins, dtype=jnp.int32)
    shifts = jnp.arange(lag_count, dtype=jnp.int32) - lag_count // 2
    phase = jnp.mod(freqs[:, None] * shifts[None, :], 2 * bins)
    angle = phase.astype(jnp.float32) * (math.pi / bins)
    return jnp.concatenate([jnp.cos(angle), -jnp.sin(angle)], axis=0).astype(jnp.bfloat16)


def day_cross(own, other, bins):
    own_re, own_im = (own[..., :bins], own[..., bins:])
    oth_re, oth_im = (other[..., :bins], other[..., bins:])
    cross_re = jnp.einsum("iwf,jwf->ijf", own_re, oth_re, preferred_element_type=jnp.float32)
    cross_re = cross_re + jnp.einsum(
        "iwf,jwf->ijf", own_im, oth_im, preferred_element_type=jnp.float32
    )
    cross_im = jnp.einsum("iwf,jwf->ijf", own_im, oth_re, preferred_element_type=jnp.float32)
    cross_im = cross_im - jnp.einsum(
        "iwf,jwf->ijf", own_re, oth_im, preferred_element_type=jnp.float32
    )
    cross = jnp.concatenate([cross_re, cross_im], axis=-1).astype(jnp.bfloat16)
    return cross.astype(jnp.float32)


def apply_lags(summed, table, norm):
    kept = summed.astype(jnp.bfloat16)
    rows = kept.shape[0] * kept.shape[1]
    lagged = (
        jnp.dot(kept.reshape(rows, kept.shape[2]), table, preferred_element_type=jnp.float32) * norm
    )
    return lagged.reshape(kept.shape[0], kept.shape[1], table.shape[1]).astype(jnp.bfloat16)


def local(spectra, owners):
    bins = spectra.shape[-1] // 2
    windows_all = spectra.shape[1] * lax.axis_size("day")
    white = whiten(spectra, bins)
    table = lag_table(bins, LAGS)
    norm = 1.0 / math.sqrt(windows_all * bins)
    result_steps = []
    for step in range(STEPS):
        block = broadcast(white, "chan", owners[step])
        crossed = day_cross(white, block, bins)
        summed = lax.psum_scatter(
            crossed.astype(jnp.bfloat16), "day", scatter_dimension=0, tiled=True
        ).astype(jnp.float32)
        result_steps.append(apply_lags(summed, table, norm))
    return jnp.stack(result_steps, axis=0)


def solution(mesh):
    placed = (P("chan", "day", None), P())
    return jax.shard_map(
        local,
        mesh=mesh,
        in_specs=placed,
        out_specs=P(None, ("chan", "day"), None, None),
        check_vma=False,
    )
```

profile of v0, /device:TPU:1, one launch (start us, length us, event | category | flops | bytes accessed | tf_op | source)
XLA Modules:
  0.0 1449.7 jit_solution(18093776150221428360)
XLA Ops:
  6.5 0.0 all-reduce.3.cloned.1.call-start
  6.5 1.5 convert_element_type.46
  8.0 0.5 fusion.13
  8.6 0.6 multiply_convert_fusion.1
  9.2 0.0 copy-start.11
  9.2 0.0 copy-start.12
  9.2 0.0 copy-start.14
  9.2 0.8 copy-done.11
  10.0 0.2 copy-done.12
  10.2 1.4 pad_maximum_fusion
  11.6 3.7 copy.11
  15.2 0.0 copy-done.14
  15.3 0.7 fusion.14
  17.3 3.2 broadcast_select_fusion.1
  20.4 0.0 copy-start.13
  20.4 0.0 all-reduce.3.cloned.1.call-update
  20.4 0.0 reduce-scatter.3.cloned.1.call-start
  20.5 1.0 copy-done.13
  21.5 1.5 copy.12
  22.9 0.0 copy-start.4
  23.0 2.6 copy.13
  25.5 0.0 copy-start.6
  25.5 1304.0 %all-reduce.3.cloned.1.call-done = (bf16[32,32,400]{1,0,2:T(8,128)(2,1)}, bf16[32,32,400]{1,0,2:T(8,128)(2,1)}) async-done(((bf16[32,32,400]{1,0,2:T(8,128)(2,1)}, bf16[32,32,400]{1,0,2:T(8,128)(2,1)}), (bf16[32,32,400]{1,0,2:T(8,128)(2,1)}, bf16[32,32,400]{1,0,2:T(8,128)(2,1)})) %all-reduce.3.cloned.1.call-update) | async-done | bytes 1638416 | tf_op jit(solution)/shard_map/psum | solution.py:14
  1329.5 0.0 copy-start.2
  1329.5 4.2 fusion.15
  1333.8 0.0 copy-done.6
  1333.8 0.0 copy-done.2
  1333.8 0.0 copy-start
  1333.8 2.7 fusion.16
  1336.4 0.0 copy-done.4
  1336.4 0.0 copy-done
  1336.4 0.0 copy-start.7
  1336.4 2.7 fusion.17
  1339.2 0.0 copy-done.7
  1339.2 2.7 fusion.18
  1341.9 0.0 copy-done.3
  1341.9 1.4 copy-done.9
  1343.3 2.1 fusion
  1345.4 3.8 copy.16
  1349.2 4.6 fusion.1
  1353.8 4.0 copy.17
  1357.8 2.6 pad_maximum_fusion.1
  1360.4 0.0 reduce-scatter.3.cloned.1.call-update
  1360.4 0.2 reduce-scatter.5.cloned.1.call-start
  1360.6 0.0 copy-done.1
  1360.7 0.0 copy-start.5
  1360.7 0.0 copy-start.8
  1360.7 4.7 fusion.2
  1365.4 0.0 copy-done.5
  1365.4 0.0 copy-done.8
  1365.4 2.1 fusion.3
  1367.5 3.3 copy.24
  1370.8 0.0 copy-done.10
  1370.9 1.9 copy.25
  1372.7 1.4 pad_maximum_fusion.2
  1374.1 0.0 reduce-scatter.5.cloned.1.call-update
  1374.2 1.8 cosine_convert_fusion
  1375.9 24.7 %reduce-scatter.3.cloned.1.call-done = bf16[16,32,400]{2,1,0:T(8,128)(2,1)} async-done(((bf16[32,32,400]{2,1,0:T(8,128)(2,1)}), bf16[16,32,400]{2,1,0:T(8,128)(2,1)}) %reduce-scatter.3.cloned.1.call-update) | async-done | bytes 409616 | tf_op jit(solution)/shard_map/reduce_scatter | solution.py:69
  1400.6 1.5 fusion.4
  1402.1 0.2 copy.18
  1402.3 38.1 %reduce-scatter.5.cloned.1.call-done = bf16[16,32,400]{2,1,0:T(8,128)(2,1)} async-done(((bf16[32,32,400]{2,1,0:T(8,128)(2,1)}), bf16[16,32,400]{2,1,0:T(8,128)(2,1)}) %reduce-scatter.5.cloned.1.call-update) | async-done | bytes 409616 | tf_op jit(solution)/shard_map/reduce_scatter | solution.py:69
  1440.4 1.5 fusion.5
  1441.9 0.2 copy.26
  1442.1 1.1 pad_maximum_fusion.3
  (6 shorter events, 0.0 us)
Async XLA Ops:
  6.5 1323.0 %all-reduce.3.cloned.1.call-start = ((), (), s32[]{:S(2)}) async-start(), calls=%async_computation.4 | async-start | bytes 13107200 | tf_op jit(solution)/shard_map/psum | solution.py:14
  9.2 0.8 copy-start.11
  9.2 1.0 copy-start.12
  9.2 6.0 copy-start.14
  20.4 1.0 copy-start.13
  20.4 1380.2 %reduce-scatter.3.cloned.1.call-start = ((), (), s32[]{:S(2)}) async-start(), calls=%async_computation.2 | async-start | bytes 1572864 | tf_op jit(solution)/shard_map/reduce_scatter | solution.py:69
  22.9 1313.5 %copy-start.4 = (bf16[32,32,200]{1,0,2:T(8,128)(2,1)}, bf16[32,32,200]{1,0,2:T(8,128)(2,1)S(1)}, u32[]{:S(2)}) copy-start(bf16[32,32,200]{1,0,2:T(8,128)(2,1)S(1)} %copy.12) | copy-start | bytes 1228804
  25.5 1308.2 %copy-start.6 = (bf16[32,32,200]{1,0,2:T(8,128)(2,1)}, bf16[32,32,200]{1,0,2:T(8,128)(2,1)S(1)}, u32[]{:S(2)}) copy-start(bf16[32,32,200]{1,0,2:T(8,128)(2,1)S(1)} %copy.13) | copy-start | bytes 1228804
  1329.5 4.2 copy-start.2
  1333.8 2.7 copy-start
  1336.4 2.7 copy-start.7
  1339.2 2.7 copy-start.3
  1339.2 4.1 copy-start.9
  1353.8 6.9 copy-start.1
  1360.4 80.0 %reduce-scatter.5.cloned.1.call-start = ((), (), s32[]{:S(2)}) async-start(), calls=%async_computation.3 | async-start | bytes 1572864 | tf_op jit(solution)/shard_map/reduce_scatter | solution.py:69
  1360.7 4.7 copy-start.5
  1360.7 4.7 copy-start.8
  1367.5 3.3 copy-start.10
Sparse Core Ops, SparseCore 0:
  20.6 1308.9 all-reduce.2
  1360.5 40.0 reduce-scatter.2
  1403.1 37.2 reduce-scatter.4
where the time goes:
time: 1450 us
  waiting for transfers between devices  1370 us (94%)
  matrix products  28.8 us (2%)
  local copies, waits for them, and re-layouts  25.2 us (2%)
  between operations  14.7 us (1%)
    psum x1, waiting for transfers between devices, broadcast(): return lax.psum(jnp.where(mine, array, jnp.zeros_like(array)), axis)  1300 us
    reduce_scatter x2, waiting for transfers between devices, local(): lax.psum_scatter(crossed.astype(jnp.bfloat16), 'day', scatter_dimension=0...  62.8 us
  transfers between devices with their start and end apart: 3, of which 3 were waited for; matrix products, arithmetic and copies ran while one was open for 1% of the time, Pallas kernels for 0%

commit v1 on v0

v1 whole, which is shorter than its diff:
```python
import math

import jax
import jax.numpy as jnp
from jax import lax
from jax.sharding import Mesh, PartitionSpec as P

LAGS = 400
STEPS = 2
BINS = 200
SHARE = 7
PLANE = ("x", "y", "core")
SIDE = 32
ALL = ("z", "x", "y", "core")


def whiten(spectra):
    values = spectra.astype(jnp.float32)
    real_part = values[..., :BINS]
    imag_part = values[..., BINS:]
    power = real_part * real_part + imag_part * imag_part
    mean_power = jnp.mean(power, axis=-1, keepdims=True)
    factor = lax.rsqrt(power + 0.25 * mean_power + 1e-06)
    return jnp.stack([real_part * factor, imag_part * factor], axis=-2).astype(jnp.bfloat16)


def lag_table():
    freqs = jnp.arange(BINS, dtype=jnp.int32)
    shifts = jnp.arange(LAGS, dtype=jnp.int32) - LAGS // 2
    phase = jnp.mod(freqs[:, None] * shifts[None, :], 2 * BINS)
    angle = phase.astype(jnp.float32) * (math.pi / BINS)
    return jnp.stack([jnp.cos(angle), -jnp.sin(angle)], axis=0).astype(jnp.bfloat16)


def by_bins(white):
    rows, wins = white.shape[:2]
    padded = jnp.pad(white, ((0, 0), (0, 0), (0, 0), (0, SIDE * SHARE - BINS)))
    return padded.reshape(rows, wins, 2, SIDE, SHARE).transpose(3, 4, 2, 0, 1)


def ring(shift):
    at = [(r % 4) * 2 + r // 4 for r in range(8)]
    return [(at[r], at[(r + shift) % 8]) for r in range(8)]


def hop(array, shift):
    return lax.ppermute(array, ("z", "day"), ring(shift))


def spread(array):
    rows, width = array.shape[0], array[0].size
    flat = array.reshape(rows, width // 128, 128)
    return lax.all_to_all(flat, PLANE, 0, 0, tiled=True).reshape(array.shape)


def local(spectra, owners):
    day = lax.axis_index("day")
    z_lo = lax.axis_index("z")
    half = spectra.shape[0] // 2
    theirs = lax.dynamic_slice_in_dim(spectra, (1 - day) * half, half, 0)
    other_raw = lax.ppermute(theirs.reshape(-1, 128), "day", [(0, 1), (1, 0)]).reshape(theirs.shape)

    own = spread(by_bins(whiten(spectra)))
    pieces = []
    for step in range(STEPS):
        piece = lax.dynamic_index_in_dim(own, owners[step] % SIDE, 0, keepdims=False)
        pieces.append(jnp.where(owners[step] // SIDE == z_lo, piece, jnp.zeros_like(piece)))
    held = jnp.stack(pieces)
    shape = held.shape
    held = held.reshape(STEPS, -1, 128)
    near = held + hop(held, 1) + hop(held, -1)
    below, above = hop(near, 3), hop(near, -3)
    ring_at = day * 4 + z_lo
    blocks = []
    for which in range(2):
        chosen = []
        for step in range(STEPS):
            home = owners[step] // SIDE + 4 * which
            delta = jnp.mod(ring_at - home + 16, 8)
            chosen.append(
                jnp.where(
                    (delta == 7) | (delta <= 1),
                    near[step],
                    jnp.where(delta <= 4, below[step], above[step]),
                )
            )
        blocks.append(jnp.stack(chosen))
    mine = jnp.where(day == 0, blocks[0], blocks[1]).reshape(shape)
    other = jnp.where(day == 0, blocks[1], blocks[0]).reshape(shape)

    other_rows = spread(by_bins(whiten(other_raw)))
    own_rows = lax.dynamic_slice_in_dim(own, day * half, half, 3)
    left = jnp.concatenate([own_rows, other_rows], axis=-1)
    right = jnp.concatenate([mine, other], axis=-1)
    product = jnp.einsum("akpiw,skcjw->kaipcsj", left, right, preferred_element_type=jnp.float32)
    real_part = product[:, :, :, 0, 0] + product[:, :, :, 1, 1]
    imag_part = product[:, :, :, 1, 0] - product[:, :, :, 0, 1]
    cross = jnp.stack([real_part, imag_part], axis=3).astype(jnp.bfloat16)
    home_rows = spread(cross.transpose(1, 0, 2, 3, 4, 5))
    summed = home_rows.reshape((SIDE * SHARE,) + home_rows.shape[2:])[:BINS]
    norm = 1.0 / math.sqrt(2 * spectra.shape[1] * BINS)
    lagged = jnp.einsum("ficsj,cfl->sijl", summed, lag_table(), preferred_element_type=jnp.float32)
    return (lagged * norm).astype(jnp.bfloat16)


def solution(mesh):
    fine = Mesh(mesh.devices.reshape(4, 4, 4, 2, 2), ALL + ("day",))
    return jax.shard_map(
        local,
        mesh=fine,
        in_specs=(P(ALL, "day", None), P()),
        out_specs=P(None, ALL + ("day",), None, None),
        check_vma=False,
    )
```

time: 1450 us -> 143 us (0.10)
  waiting for transfers between devices: 1370 us -> 24.5 us
  starting transfers between devices: 0.27 us -> 34.9 us
  local copies, waits for them, and re-layouts: 25.2 us -> 58.7 us
  matrix products: 28.8 us -> 6.92 us
    psum x1 -> x0, waiting for transfers between devices: 1300 us -> none  [broadcast(): return lax.psum(jnp.where(mine, array, jnp.zeros_like(array)), axis)]
    reduce_scatter x2 -> x0, waiting for transfers between devices: 62.8 us -> none  [local(): lax.psum_scatter(crossed.astype(jnp.bfloat16), 'day', scatter_dimension=0...]
    reshape x0 -> x7, local copies, waits for them, and re-layouts: none -> 26 us  [the longest x3 14.9 us: spread(): flat = array.reshape(rows, width // 128, 128)]
    all_to_all x0 -> x3, waiting for transfers between devices: none -> 22.9 us  [spread(): return lax.all_to_all(flat, PLANE, 0, 0, tiled=True).reshape(array.shape)]
    dot_general x10 -> x2, matrix products: 28.8 us -> 6.92 us  [the longest x1 4.53 us: local(): jnp.einsum('akpiw,skcjw->kaipcsj', left, right, preferred_element_type=jn...]
    all_to_all x0 -> x3, starting transfers between devices: none -> 19.8 us  [spread(): return lax.all_to_all(flat, PLANE, 0, 0, tiled=True).reshape(array.shape)]
    ppermute x0 -> x5, starting transfers between devices: none -> 15 us  [the longest x1 7.74 us: local(): lax.ppermute(theirs.reshape(-1, 128), 'day', [(0, 1), (1, 0)])]
  transfers between devices with their start and end apart: 3 -> 8, of which waited for: 3 -> 3; matrix products, arithmetic and copies ran while one was open for 1% -> 26% of each run, Pallas kernels for 0% -> 0%
where the time goes in v1:
time: 143 us; the launch traced here: 141 us
  local copies, waits for them, and re-layouts  58.7 us (41%)
  starting transfers between devices  34.9 us (24%)
  waiting for transfers between devices  24.5 us (17%)
  other arithmetic  11.4 us (8%)
  matrix products  6.92 us (5%)
  between operations  5.17 us (4%)
    all_to_all x3, waiting for transfers between devices, spread(): return lax.all_to_all(flat, PLANE, 0, 0, tiled=True).reshape(array.shape)  22.9 us
    all_to_all x3, starting transfers between devices, spread(): return lax.all_to_all(flat, PLANE, 0, 0, tiled=True).reshape(array.shape)  19.8 us
    reshape x3, local copies, waits for them, and re-layouts, spread(): flat = array.reshape(rows, width // 128, 128)  14.9 us
    transpose x1, local copies, waits for them, and re-layouts, local(): home_rows = spread(cross.transpose(1, 0, 2, 3, 4, 5))  11.6 us
    reshape x3, local copies, waits for them, and re-layouts, spread(): return lax.all_to_all(flat, PLANE, 0, 0, tiled=True).reshape(array.shape)  9.19 us
    ppermute x1, starting transfers between devices, local(): lax.ppermute(theirs.reshape(-1, 128), 'day', [(0, 1), (1, 0)])  7.74 us
    ppermute x4, starting transfers between devices, hop(): return lax.ppermute(array, ('z', 'day'), ring(shift))  7.31 us
    unnamed x10, local copies, waits for them, and re-layouts  7.17 us
  transfers between devices with their start and end apart: 8, of which 3 were waited for; matrix products, arithmetic and copies ran while one was open for 26% of the time, Pallas kernels for 0%

profile of v1, /device:TPU:1, one launch (start us, length us, event | category | flops | bytes accessed | tf_op | source)
XLA Modules:
  0.0 141.5 jit_solution(6604101484988015814)
XLA Ops:
  0.0 1.1 constant_dynamic-slice_fusion
  1.1 1.9 %reshape.180 = bf16[1600,128]{1,0:T(8,128)(2,1)} reshape(bf16[16,32,400]{2,1,0:T(8,128)(2,1)S(1)} %constant_dynamic-slice_fusion) | data formatting | bytes 819200 | tf_op jit(solution)/shard_map/reshape | solution.py:61
  2.9 7.7 %collective-permute-start.4 = (bf16[1600,128]{1,0:T(8,128)(2,1)}, bf16[1600,128]{1,0:T(8,128)(2,1)}, u32[]{:S(2)}, u32[]{:S(2)}) collective-permute-start(bf16[1600,128]{1,0:T(8,128)(2,1)} %reshape.180), channel_id=1, source_target_pairs={{0,1},{1,0},{2,3},{3,2},{4,5},{5,4},{6,7},{7,6},{8,9},{9,8},{10,11... | collective-permute-start | bytes 1228808 | tf_op jit(solution)/shard_map/ppermute | solution.py:61
  10.7 3.7 %copy.39 = bf16[32,32,400]{1,0,2:T(8,128)(2,1)S(1)} copy(bf16[32,32,400]{2,1,0:T(8,128)(2,1)} %param.2) | data formatting | bytes 1638400 | tf_op args[0]
  14.4 0.9 convert_element_type.40
  15.3 0.6 fusion.34
  15.9 1.1 fusion.13
  17.0 0.7 fusion.2
  17.8 2.8 %copy.40 = bf16[32,7,2,32,32]{4,3,2,1,0:T(8,128)(2,1)} copy(bf16[32,7,2,32,32]{4,3,1,0,2:T(8,128)(2,1)S(1)} %bitcast.70) | data formatting | bytes 1835008 | tf_op jit(solution)/shard_map/transpose | solution.py:38
  20.6 5.4 %reshape.178 = bf16[32,112,128]{2,1,0:T(8,128)(2,1)} reshape(bf16[32,7,2,32,32]{4,3,2,1,0:T(8,128)(2,1)} %copy.40) | data formatting | bytes 1835008 | tf_op jit(solution)/shard_map/reshape | solution.py:52
  26.0 8.1 %all-to-all-start = ((bf16[32,112,128]{2,1,0:T(8,128)(2,1)}), bf16[32,112,128]{2,1,0:T(8,128)(2,1)}, u32[]{:S(2)}, u32[]{:S(2)}) async-start(bf16[32,112,128]{2,1,0:T(8,128)(2,1)} %reshape.178), calls=%async_computation | async-start | bytes 1835008 | tf_op jit(solution)/shard_map/all_to_all | solution.py:53
  34.1 0.0 collective-permute-done.4
  34.1 2.1 %reshape.185 = f32[16,32,400]{2,1,0:T(8,128)S(1)} reshape(bf16[1600,128]{1,0:T(8,128)(2,1)} %collective-permute-done.4) | data formatting | bytes 1228800 | tf_op jit(solution)/shard_map/convert_element_type | solution.py:18
  36.2 0.3 fusion.33
  36.6 0.3 fusion.27
  36.9 0.1 pad_maximum_fusion
  37.0 1.5 %copy.59 = bf16[16,32,2,200]{1,0,2,3:T(8,128)(2,1)S(1)} copy(bf16[16,32,2,200]{3,1,0,2:T(8,128)(2,1)S(1)} %pad_maximum_fusion) | data formatting | bytes 819200
  38.5 0.0 copy-start.1
  38.5 0.3 pad.9.clone
  38.8 1.6 %reshape.182 = bf16[32,56,128]{2,1,0:T(8,128)(2,1)} reshape(bf16[32,7,2,16,32]{4,3,2,1,0:T(8,128)(2,1)S(1)} %bitcast.71) | data formatting | bytes 917504 | tf_op jit(solution)/shard_map/reshape | solution.py:52
  40.5 9.2 %all-to-all-done = bf16[32,112,128]{2,1,0:T(8,128)(2,1)} async-done(((bf16[32,112,128]{2,1,0:T(8,128)(2,1)}), bf16[32,112,128]{2,1,0:T(8,128)(2,1)}, u32[]{:S(2)}, u32[]{:S(2)}) %all-to-all-start) | async-done | bytes 917536 | tf_op jit(solution)/shard_map/all_to_all | solution.py:53
  49.7 4.0 %all-to-all-start.1 = ((bf16[32,56,128]{2,1,0:T(8,128)(2,1)}), bf16[32,56,128]{2,1,0:T(8,128)(2,1)S(1)}, u32[]{:S(2)}, u32[]{:S(2)}) async-start(bf16[32,56,128]{2,1,0:T(8,128)(2,1)} %reshape.182), calls=%async_computation.1 | async-start | bytes 917504 | tf_op jit(solution)/shard_map/all_to_all | solution.py:53
  53.7 0.0 copy-done.1
  53.7 0.6 fusion.35
  59.1 5.1 %reshape.179 = bf16[32,7,2,32,32]{4,3,2,1,0:T(8,128)(2,1)} reshape(bf16[32,112,128]{2,1,0:T(8,128)(2,1)} %all-to-all-done) | data formatting | bytes 1835008 | tf_op jit(solution)/shard_map/reshape | solution.py:53
  64.2 1.0 dynamic-slice_select_fusion
  65.2 0.1 stack.67
  65.3 0.1 stack.68
  65.5 0.8 collective-permute-start
  66.3 1.9 %collective-permute-start.1 = (bf16[2,112,128]{2,1,0:T(8,128)(2,1)S(1)}, bf16[2,112,128]{2,1,0:T(8,128)(2,1)S(1)}, u32[]{:S(2)}, u32[]{:S(2)}) collective-permute-start(bf16[2,112,128]{2,1,0:T(8,128)(2,1)S(1)} %constant_dynamic-update-slice_fusion), channel_id=1, source_target_pairs={{0,193},{64,0},{128,64},{192,128},{1,192},{65,1},{129,65},{193,129... | collective-permute-start | bytes 172040 | tf_op jit(solution)/shard_map/ppermute | solution.py:47
  68.2 0.0 all-to-all-done.1
  68.2 1.7 %reshape.183 = bf16[32,7,2,16,32]{4,3,2,1,0:T(8,128)(2,1)} reshape(bf16[32,56,128]{2,1,0:T(8,128)(2,1)S(1)} %all-to-all-done.1) | data formatting | bytes 917504 | tf_op jit(solution)/shard_map/reshape | solution.py:53
  69.9 0.0 copy-start
  69.9 2.4 %copy.44 = bf16[32,7,2,16,32]{4,0,3,2,1:T(8,128)(2,1)S(1)} copy(bf16[32,7,2,16,32]{4,3,2,1,0:T(8,128)(2,1)} %reshape.183) | data formatting | bytes 917504 | tf_op jit(solution)/shard_map/reshape | solution.py:53
  72.3 0.0 collective-permute-done
  72.3 0.0 collective-permute-done.1
  72.3 0.5 collective-permute-start.2
  72.8 4.0 %collective-permute-start.3 = (bf16[2,112,128]{2,1,0:T(8,128)(2,1)S(1)}, bf16[2,112,128]{2,1,0:T(8,128)(2,1)S(1)}, u32[]{:S(2)}, u32[]{:S(2)}) collective-permute-start(bf16[2,112,128]{2,1,0:T(8,128)(2,1)S(1)} %add_add_fusion), channel_id=1, source_target_pairs={{0,65},{64,129},{128,193},{192,0},{1,64},{65,128},{129,192},{193,1... | collective-permute-start | bytes 172040 | tf_op jit(solution)/shard_map/ppermute | solution.py:47
  76.9 0.0 copy-done
  76.9 0.4 constant_dynamic-slice_fusion.1
  77.3 2.0 %copy.55 = bf16[32,7,2,16,32]{4,0,3,2,1:T(8,128)(2,1)} copy(bf16[32,7,2,16,32]{4,3,2,1,0:T(8,128)(2,1)S(1)} %constant_dynamic-slice_fusion.1) | data formatting | bytes 917504
  79.3 1.6 %collective-permute-done.2 = bf16[2,112,128]{2,1,0:T(8,128)(2,1)S(1)} collective-permute-done((bf16[2,112,128]{2,1,0:T(8,128)(2,1)S(1)}, bf16[2,112,128]{2,1,0:T(8,128)(2,1)S(1)}, u32[]{:S(2)}, u32[]{:S(2)}) %collective-permute-start.2) | collective-permute-done | bytes 57376 | tf_op jit(solution)/shard_map/ppermute | solution.py:47
  80.9 0.0 collective-permute-done.3
  80.9 0.1 stack.73
  81.0 0.1 stack.71
  81.1 0.1 stack.74
  81.3 0.1 stack.70
  81.5 4.5 %convolution_bitcast_fusion = f32[7,32,16,2,2,2,32]{1,6,2,3,4,5,0:T(8,128)S(1)} fusion(bf16[32,7,2,16,32]{4,0,3,2,1:T(8,128)(2,1)S(1)} %copy.44, bf16[32,7,2,16,32]{4,0,3,2,1:T(8,128)(2,1)} %copy.55, bf16[2,7,2,32,32]{4,3,2,0,1:T(8,128)(2,1)S(1)} %get-tuple-element.12, bf16[2,7,2,32,32]{4,3,2,0,1:T(8,128)(2,1)S(1)} %get-tuple-element.11), kind=kOutput, calls=%fused_computation | convolution fusion | flops 119504896 | bytes 4702208 | tf_op jit(solution)/shard_map/akpiw,skcjw->kaipcsj/dot_general | solution.py:95
  86.0 0.9 fusion.10
  86.9 0.9 fusion.9
  87.8 2.6 %maximum_bitcast_fusion = bf16[32,7,16,2,2,32]{0,5,2,4,1,3:T(8,128)(2,1)} fusion(bf16[7,32,16,1,2,32]{1,5,2,4,0,3:T(8,128)(2,1)S(1)} %fusion.10, bf16[7,32,16,1,2,32]{1,5,2,4,0,3:T(8,128)(2,1)S(1)} %fusion.9), kind=kLoop, calls=%fused_computation.11 | loop fusion | flops 458752 | bytes 1835008 | tf_op jit(solution)/shard_map/transpose | solution.py:99
  90.4 11.6 %copy.47 = bf16[32,7,16,2,2,32]{5,4,3,2,1,0:T(2,128)(2,1)} copy(bf16[32,7,16,2,2,32]{0,5,2,4,1,3:T(8,128)(2,1)} %maximum_bitcast_fusion) | data formatting | bytes 1835008 | tf_op jit(solution)/shard_map/transpose | solution.py:99
  102.0 7.8 %reshape.184 = bf16[32,112,128]{2,1,0:T(8,128)(2,1)} reshape(bf16[32,7,16,2,2,32]{5,4,3,2,1,0:T(2,128)(2,1)} %copy.47) | data formatting | bytes 1835008 | tf_op jit(solution)/shard_map/reshape | solution.py:52
  109.8 7.8 %all-to-all-start.2 = ((bf16[32,112,128]{2,1,0:T(8,128)(2,1)}), bf16[32,112,128]{2,1,0:T(8,128)(2,1)S(1)}, u32[]{:S(2)}, u32[]{:S(2)}) async-start(bf16[32,112,128]{2,1,0:T(8,128)(2,1)} %reshape.184), calls=%async_computation.2 | async-start | bytes 1835008 | tf_op jit(solution)/shard_map/all_to_all | solution.py:53
  117.6 1.8 %cosine_convert_fusion = (bf16[1,200,400]{2,1,0:T(8,128)(2,1)S(1)}, bf16[1,200,400]{2,1,0:T(8,128)(2,1)S(1)}) fusion(s32[400]{0:T(512)S(1)} %iota_add_fusion), kind=kLoop, calls=%fused_computation.40 | loop fusion | flops 960000 | bytes 321600 | tf_op jit(solution)/shard_map/convert.13
  119.4 13.7 %all-to-all-done.2 = bf16[32,112,128]{2,1,0:T(8,128)(2,1)S(1)} async-done(((bf16[32,112,128]{2,1,0:T(8,128)(2,1)}), bf16[32,112,128]{2,1,0:T(8,128)(2,1)S(1)}, u32[]{:S(2)}, u32[]{:S(2)}) %all-to-all-start.2) | async-done | bytes 917536 | tf_op jit(solution)/shard_map/all_to_all | solution.py:53
  133.1 3.0 %reshape_reshape.3 = bf16[224,16,2,2,32]{4,3,2,1,0:T(2,128)(2,1)} reshape(bf16[32,112,128]{2,1,0:T(8,128)(2,1)S(1)} %all-to-all-done.2) | data formatting | bytes 1835008 | tf_op jit(solution)/shard_map/reshape;reshape | solution.py:100
  136.1 0.0 slice-start
  136.1 1.9 %slice-done = bf16[200,16,2,2,32]{4,3,2,1,0:T(2,128)(2,1)S(1)} async-done(((bf16[224,16,2,2,32]{4,3,2,1,0:T(2,128)(2,1)}), bf16[200,16,2,2,32]{4,3,2,1,0:T(2,128)(2,1)S(1)}, s32[]{:S(2)}) %slice-start) | async-done | bytes 819224 | tf_op jit(solution)/shard_map/slice | solution.py:100
  138.0 2.4 %fusion.17 = bf16[2,16,32,400]{3,2,0,1:T(8,128)(2,1)S(1)} fusion(bf16[200,16,2,2,32]{4,3,2,1,0:T(2,128)(2,1)S(1)} %slice-done, bf16[1,200,400]{2,1,0:T(8,128)(2,1)S(1)} %get-tuple-element.17, bf16[1,200,400]{2,1,0:T(8,128)(2,1)S(1)} %get-tuple-element.16), kind=kOutput, calls=%fused_computation.27 | convolution fusion | flops 329139200 | bytes 1958400 | tf_op jit(solution)/shard_map/ficsj,cfl->sijl/dot_general | solution.py:102
  140.4 1.0 copy.49
  (12 shorter events, 0.2 us)
Async XLA Ops:
  2.9 31.2 %collective-permute-start.4 = (bf16[1600,128]{1,0:T(8,128)(2,1)}, bf16[1600,128]{1,0:T(8,128)(2,1)}, u32[]{:S(2)}, u32[]{:S(2)}) collective-permute-start(bf16[1600,128]{1,0:T(8,128)(2,1)} %reshape.180), channel_id=1, source_target_pairs={{0,1},{1,0},{2,3},{3,2},{4,5},{5,4},{6,7},{7,6},{8,9},{9,8},{10,11... | collective-permute-start | bytes 1228808 | tf_op jit(solution)/shard_map/ppermute | solution.py:61
  26.0 23.6 %all-to-all-start = ((bf16[32,112,128]{2,1,0:T(8,128)(2,1)}), bf16[32,112,128]{2,1,0:T(8,128)(2,1)}, u32[]{:S(2)}, u32[]{:S(2)}) async-start(bf16[32,112,128]{2,1,0:T(8,128)(2,1)} %reshape.178), calls=%async_computation | async-start | bytes 1835008 | tf_op jit(solution)/shard_map/all_to_all | solution.py:53
  38.5 15.2 %copy-start.1 = (s32[2]{0:T(128)S(1)}, s32[2]{0:T(128)}, u32[]{:S(2)}) copy-start(s32[2]{0:T(128)} %param.3) | copy-start | bytes 28
  49.7 18.5 %all-to-all-start.1 = ((bf16[32,56,128]{2,1,0:T(8,128)(2,1)}), bf16[32,56,128]{2,1,0:T(8,128)(2,1)S(1)}, u32[]{:S(2)}, u32[]{:S(2)}) async-start(bf16[32,56,128]{2,1,0:T(8,128)(2,1)} %reshape.182), calls=%async_computation.1 | async-start | bytes 917504 | tf_op jit(solution)/shard_map/all_to_all | solution.py:53
  65.5 6.8 %collective-permute-start = (bf16[2,112,128]{2,1,0:T(8,128)(2,1)S(1)}, bf16[2,112,128]{2,1,0:T(8,128)(2,1)S(1)}, u32[]{:S(2)}, u32[]{:S(2)}) collective-permute-start(bf16[2,112,128]{2,1,0:T(8,128)(2,1)S(1)} %constant_dynamic-update-slice_fusion), channel_id=1, source_target_pairs={{0,64},{64,128},{128,192},{192,1},{1,65},{65,129},{129,193},{193,0... | collective-permute-start | bytes 172040 | tf_op jit(solution)/shard_map/ppermute | solution.py:47
  66.3 6.0 %collective-permute-start.1 = (bf16[2,112,128]{2,1,0:T(8,128)(2,1)S(1)}, bf16[2,112,128]{2,1,0:T(8,128)(2,1)S(1)}, u32[]{:S(2)}, u32[]{:S(2)}) collective-permute-start(bf16[2,112,128]{2,1,0:T(8,128)(2,1)S(1)} %constant_dynamic-update-slice_fusion), channel_id=1, source_target_pairs={{0,193},{64,0},{128,64},{192,128},{1,192},{65,1},{129,65},{193,129... | collective-permute-start | bytes 172040 | tf_op jit(solution)/shard_map/ppermute | solution.py:47
  69.9 7.0 %copy-start = (bf16[32,7,2,32,32]{4,3,2,1,0:T(8,128)(2,1)S(1)}, bf16[32,7,2,32,32]{4,3,2,1,0:T(8,128)(2,1)}, u32[]{:S(2)}) copy-start(bf16[32,7,2,32,32]{4,3,2,1,0:T(8,128)(2,1)} %reshape.179) | copy-start | bytes 2752516
  72.3 8.5 %collective-permute-start.2 = (bf16[2,112,128]{2,1,0:T(8,128)(2,1)S(1)}, bf16[2,112,128]{2,1,0:T(8,128)(2,1)S(1)}, u32[]{:S(2)}, u32[]{:S(2)}) collective-permute-start(bf16[2,112,128]{2,1,0:T(8,128)(2,1)S(1)} %add_add_fusion), channel_id=1, source_target_pairs={{0,192},{64,1},{128,65},{192,129},{1,193},{65,0},{129,64},{193,128... | collective-permute-start | bytes 172040 | tf_op jit(solution)/shard_map/ppermute | solution.py:47
  72.8 8.0 %collective-permute-start.3 = (bf16[2,112,128]{2,1,0:T(8,128)(2,1)S(1)}, bf16[2,112,128]{2,1,0:T(8,128)(2,1)S(1)}, u32[]{:S(2)}, u32[]{:S(2)}) collective-permute-start(bf16[2,112,128]{2,1,0:T(8,128)(2,1)S(1)} %add_add_fusion), channel_id=1, source_target_pairs={{0,65},{64,129},{128,193},{192,0},{1,64},{65,128},{129,192},{193,1... | collective-permute-start | bytes 172040 | tf_op jit(solution)/shard_map/ppermute | solution.py:47
  109.8 23.3 %all-to-all-start.2 = ((bf16[32,112,128]{2,1,0:T(8,128)(2,1)}), bf16[32,112,128]{2,1,0:T(8,128)(2,1)S(1)}, u32[]{:S(2)}, u32[]{:S(2)}) async-start(bf16[32,112,128]{2,1,0:T(8,128)(2,1)} %reshape.184), calls=%async_computation.2 | async-start | bytes 1835008 | tf_op jit(solution)/shard_map/all_to_all | solution.py:53
  136.1 1.9 %slice-start = ((bf16[224,16,2,2,32]{4,3,2,1,0:T(2,128)(2,1)}), bf16[200,16,2,2,32]{4,3,2,1,0:T(2,128)(2,1)S(1)}, s32[]{:S(2)}) async-start(bf16[224,16,2,2,32]{4,3,2,1,0:T(2,128)(2,1)} %reshape_reshape.3), calls=%async_computation.3 | async-start | bytes 6553600 | tf_op jit(solution)/shard_map/slice | solution.py:100

commit v2 on v1

v2 whole, which is shorter than its diff:
```python
import math

import jax
import jax.numpy as jnp
from jax import lax
from jax.experimental import pallas as pl
from jax.experimental.pallas import tpu as pltpu
from jax.sharding import Mesh, PartitionSpec as P

LAGS = 400
STEPS = 2
BINS = 200
SHARE = 7
SIDE = 32
PLANE = ("x", "y", "core")
ALL = ("z", "x", "y", "core")
ROWS = SHARE * 16
HALF = SHARE * 8
VMEM = pl.BlockSpec(memory_space=pltpu.VMEM)
SMEM = pl.BlockSpec(memory_space=pltpu.SMEM)
ROOM = pltpu.CompilerParams(vmem_limit_bytes=48 * 1024 * 1024)


def lag_table():
    freqs = jnp.arange(BINS, dtype=jnp.int32)
    shifts = jnp.arange(LAGS, dtype=jnp.int32) - LAGS // 2
    phase = jnp.mod(freqs[:, None] * shifts[None, :], 2 * BINS)
    angle = phase.astype(jnp.float32) * (math.pi / BINS)
    return jnp.stack([jnp.cos(angle), -jnp.sin(angle)], axis=0).astype(jnp.bfloat16)


def prep_kernel(place_ref, spectra_ref, out_ref, theirs_ref, rows_ref):
    day = place_ref[0]
    low = lax.broadcasted_iota(jnp.int32, (BINS, 128), 1) < 64
    pad = SIDE * SHARE - BINS
    rows_ref[BINS * 16 :, :] = jnp.zeros((pad * 16, 128), jnp.float32)
    for half in range(2):
        for pair in range(4):
            parts = []
            for a in (2 * pair, 2 * pair + 1):
                for q in range(2):
                    parts.append(spectra_ref[half * 16 + q * 8 + a].astype(jnp.float32))
            turned = jnp.concatenate(parts, axis=0).T
            re, im = turned[:BINS], turned[BINS:]
            power = re * re + im * im
            mean_power = jnp.mean(power, axis=0, keepdims=True)
            factor = lax.rsqrt(power + 0.25 * mean_power + 1e-06)
            re, im = re * factor, im * factor
            first = jnp.where(low, re, pltpu.roll(im, 64, 1))
            second = jnp.where(low, pltpu.roll(re, 64, 1), im)
            at = half * 8 + 2 * pair
            rows_ref[pl.ds(at, BINS, stride=16), :] = first
            rows_ref[pl.ds(at + 1, BINS, stride=16), :] = second
    for dest in range(SIDE):
        chunk = rows_ref[dest * ROWS : (dest + 1) * ROWS, :]
        out_ref[dest] = chunk.astype(jnp.bfloat16)
        split = chunk.reshape(SHARE, 2, 8, 128)
        theirs = jnp.where(day == 0, split[:, 1], split[:, 0])
        theirs_ref[dest] = theirs.reshape(HALF, 128).astype(jnp.bfloat16)


def prep(place, spectra):
    return pl.pallas_call(
        prep_kernel,
        out_shape=(
            jax.ShapeDtypeStruct((SIDE, ROWS, 128), jnp.bfloat16),
            jax.ShapeDtypeStruct((SIDE, HALF, 128), jnp.bfloat16),
        ),
        in_specs=[SMEM, VMEM],
        out_specs=(VMEM, VMEM),
        scratch_shapes=[pltpu.VMEM((SIDE * ROWS, 128), jnp.float32)],
        compiler_params=ROOM,
        name="prep",
    )(place, spectra)


def weights(value):
    lane = lax.broadcasted_iota(jnp.int32, value.shape, 1)
    odd = (lane // 32) % 2 == 1
    zero = jnp.zeros_like(value)
    even_v, odd_v = jnp.where(odd, zero, value), jnp.where(odd, value, zero)
    at = ((even_v, pltpu.roll(odd_v, 96, 1)), (pltpu.roll(even_v, 32, 1), odd_v))
    rows = []
    for q_i in range(2):
        for c in range(2):
            parts = []
            for q_j in range(2):
                part = at[q_i][q_j]
                if c == 1:
                    part = pltpu.roll(part, 64, 1)
                    part = jnp.where(lane < 64, -part, part)
                parts.append(part)
            rows.append(
                jnp.concatenate([parts[0][:8], parts[1][:8], parts[0][8:], parts[1][8:]], axis=0)
            )
    return rows


def cross_kernel(place_ref, own_ref, other_ref, near_ref, below_ref, above_ref, out_ref):
    day, z_lo = place_ref[0], place_ref[1]
    blocks = []
    for which in range(2):
        day_of = (day + which) % 2
        chosen = []
        for step in range(STEPS):
            home = place_ref[2 + step] // SIDE + 4 * day_of
            delta = (day * 4 + z_lo - home + 16) % 8
            use_near = (delta == 7) | (delta <= 1)
            use_below = delta <= 4
            near = near_ref[step].astype(jnp.float32)
            below = below_ref[step].astype(jnp.float32)
            above = above_ref[step].astype(jnp.float32)
            chosen.append(jnp.where(use_near, near, jnp.where(use_below, below, above)))
        blocks.append(chosen)
    own_all = own_ref[...].astype(jnp.float32).reshape(SIDE, SHARE, 2, 8, 128)
    other_all = other_ref[...].astype(jnp.float32).reshape(SIDE, SHARE, 8, 128)
    for k in range(SHARE):
        sides = []
        for which in range(2):
            parts = [weights(blocks[which][step][k * 16 : k * 16 + 16]) for step in range(STEPS)]
            order = []
            for at in range(4):
                for step in range(STEPS):
                    order.append(parts[step][at])
            sides.append(jnp.concatenate(order, axis=0))
        right = jnp.concatenate(sides, axis=1).astype(jnp.bfloat16)
        own = jnp.where(day == 0, own_all[:, k, 0], own_all[:, k, 1]).reshape(SIDE * 8, 128)
        other = other_all[:, k].reshape(SIDE * 8, 128)
        left = jnp.concatenate([own, other], axis=1).astype(jnp.bfloat16)
        product = lax.dot_general(
            left, right, (((1,), (1,)), ((), ())), preferred_element_type=jnp.float32
        )
        low = product[:, :128].reshape(SIDE, 8, 128)
        high = product[:, 128:].reshape(SIDE, 8, 128)
        both = jnp.concatenate([low, high], axis=1)
        out_ref[:, k * 16 : k * 16 + 16, :] = both.astype(jnp.bfloat16)


def cross(place, own, other, near, below, above):
    return pl.pallas_call(
        cross_kernel,
        out_shape=jax.ShapeDtypeStruct((SIDE, ROWS, 128), jnp.bfloat16),
        in_specs=[SMEM] + [VMEM] * 5,
        out_specs=VMEM,
        compiler_params=ROOM,
        name="cross",
    )(place, own, other, near, below, above)


def lag_kernel(norm, summed_ref, table_ref, out_ref, rows_ref):
    rows_ref[...] = summed_ref[...].astype(jnp.float32).reshape(SIDE * ROWS, 128)
    for i in range(16):
        turned = rows_ref[pl.ds(i, BINS, stride=16), :].T.astype(jnp.bfloat16)
        lagged = jnp.dot(turned[:64], table_ref[0], preferred_element_type=jnp.float32)
        lagged = lagged + jnp.dot(turned[64:], table_ref[1], preferred_element_type=jnp.float32)
        lagged = (lagged * norm).astype(jnp.bfloat16)
        for step in range(STEPS):
            out_ref[step, i] = lagged[step * 32 : step * 32 + 32]


def lag(norm, summed, table):
    def kernel(*refs):
        lag_kernel(norm, *refs)

    return pl.pallas_call(
        kernel,
        out_shape=jax.ShapeDtypeStruct((STEPS, 16, 32, LAGS), jnp.bfloat16),
        in_specs=[VMEM, VMEM],
        out_specs=VMEM,
        scratch_shapes=[pltpu.VMEM((SIDE * ROWS, 128), jnp.float32)],
        compiler_params=ROOM,
        name="lag",
    )(summed, table)


def hop(array, shift):
    at = [(r % 4) * 2 + r // 4 for r in range(8)]
    ring = [(at[r], at[(r + shift) % 8]) for r in range(8)]
    return lax.ppermute(array, ("z", "day"), ring)


def spread(array):
    return lax.all_to_all(array, PLANE, 0, 0, tiled=True)


def local(spectra, owners):
    day = lax.axis_index("day").astype(jnp.int32)
    z_lo = lax.axis_index("z").astype(jnp.int32)
    place = jnp.concatenate([jnp.stack([day, z_lo]), owners])
    mine, theirs = prep(place, spectra)
    arrived = lax.ppermute(theirs, "day", [(0, 1), (1, 0)])
    own = spread(mine)
    pieces = []
    for step in range(STEPS):
        piece = lax.dynamic_index_in_dim(own, owners[step] % SIDE, 0, keepdims=False)
        pieces.append(jnp.where(owners[step] // SIDE == z_lo, piece, jnp.zeros_like(piece)))
    held = jnp.stack(pieces)
    near = held + hop(held, 1) + hop(held, -1)
    below, above = hop(near, 3), hop(near, -3)
    other = spread(arrived)
    home = spread(cross(place, own, other, near, below, above))
    norm = 1.0 / math.sqrt(2 * spectra.shape[1] * BINS)
    return lag(norm, home, lag_table())


def solution(mesh):
    fine = Mesh(mesh.devices.reshape(4, 4, 4, 2, 2), ALL + ("day",))
    return jax.shard_map(
        local,
        mesh=fine,
        in_specs=(P(ALL, "day", None), P()),
        out_specs=P(None, ALL + ("day",), None, None),
        check_vma=False,
    )
```

time: 143 us -> 95 us (0.66)
  local copies, waits for them, and re-layouts: 58.7 us -> 2.46 us
  starting transfers between devices: 34.9 us -> 49.8 us
  other arithmetic: 11.4 us -> 1.93 us
  Pallas kernels: 0 us -> 7.56 us
  matrix products: 6.92 us -> 0 us
  waiting for transfers between devices: 24.5 us -> 27.7 us
    reshape x7 -> x0, local copies, waits for them, and re-layouts: 26 us -> none  [the longest x3 14.9 us: spread(): flat = array.reshape(rows, width // 128, 128)]
    transpose x2 -> x0, local copies, waits for them, and re-layouts: 14.4 us -> none  [the longest x1 11.6 us: local(): home_rows = spread(cross.transpose(1, 0, 2, 3, 4, 5))]
    ppermute x5, waiting for transfers between devices: 1.59 us -> 14.1 us  [the longest x1 7.43 us: local(): arrived = lax.ppermute(theirs, 'day', [(0, 1), (1, 0)])]
    all_to_all x3, waiting for transfers between devices: 22.9 us -> 13.7 us  [spread(): return lax.all_to_all(array, PLANE, 0, 0, tiled=True)]
    all_to_all x3, starting transfers between devices: 19.8 us -> 27.5 us  [spread(): return lax.all_to_all(array, PLANE, 0, 0, tiled=True)]
    pallas_call x0 -> x3, Pallas kernels: none -> 7.56 us  [the longest x1 2.71 us: prep(): pl.pallas_call(prep_kernel, out_shape=(jax.ShapeDtypeStruct((SIDE, ROWS,...]
    ppermute x5, starting transfers between devices: 15 us -> 22.3 us  [the longest x4 15.3 us: hop(): return lax.ppermute(array, ('z', 'day'), ring)]
    dot_general x2 -> x0, matrix products: 6.92 us -> none  [the longest x1 4.53 us: local(): jnp.einsum('akpiw,skcjw->kaipcsj', left, right, preferred_element_type=jn...]
  transfers between devices with their start and end apart: 8 -> 8, of which waited for: 3 -> 5; matrix products, arithmetic and copies ran while one was open for 26% -> 3% of each run, Pallas kernels for 0% -> 0%
where the time goes in v2:
time: 95 us; the launch traced here: 94.5 us
  starting transfers between devices  49.8 us (52%)
  waiting for transfers between devices  27.7 us (29%)
  Pallas kernels  7.56 us (8%)
  between operations  5.01 us (5%)
  local copies, waits for them, and re-layouts  2.46 us (3%)
  other arithmetic  1.93 us (2%)
    all_to_all x3, starting transfers between devices, spread(): return lax.all_to_all(array, PLANE, 0, 0, tiled=True)  27.5 us
    ppermute x4, starting transfers between devices, hop(): return lax.ppermute(array, ('z', 'day'), ring)  15.3 us
    all_to_all x3, waiting for transfers between devices, spread(): return lax.all_to_all(array, PLANE, 0, 0, tiled=True)  13.7 us
    ppermute x1, waiting for transfers between devices, local(): arrived = lax.ppermute(theirs, 'day', [(0, 1), (1, 0)])  7.43 us
    ppermute x1, starting transfers between devices, local(): arrived = lax.ppermute(theirs, 'day', [(0, 1), (1, 0)])  7 us
    ppermute x4, waiting for transfers between devices, hop(): return lax.ppermute(array, ('z', 'day'), ring)  6.65 us
    pallas_call x1, Pallas kernels, prep(): pl.pallas_call(prep_kernel, out_shape=(jax.ShapeDtypeStruct((SIDE, ROWS,...  2.71 us
    pallas_call x1, Pallas kernels, lag(): pl.pallas_call(kernel, out_shape=jax.ShapeDtypeStruct((STEPS, 16, 32, LAG...  2.6 us
  transfers between devices with their start and end apart: 8, of which 5 were waited for; matrix products, arithmetic and copies ran while one was open for 3% of the time, Pallas kernels for 0%

profile of v2, /device:TPU:1, one launch (start us, length us, event | category | flops | bytes accessed | tf_op | source)
XLA Modules:
  0.0 94.5 jit_solution(14825124127335171740)
XLA Ops:
  0.0 0.0 copy-start.1
  0.0 0.7 copy-done.1
  0.7 0.1 pad_add_fusion.place_ref
  0.7 0.0 copy-start
  0.7 1.2 %copy-done = bf16[32,32,400]{2,1,0:T(8,128)(2,1)S(1)} copy-done((bf16[32,32,400]{2,1,0:T(8,128)(2,1)S(1)}, bf16[32,32,400]{2,1,0:T(8,128)(2,1)}, u32[]{:S(2)}) %copy-start) | copy-done | bytes 819224
  2.0 2.7 %prep.1 = (bf16[32,112,128]{2,1,0:T(8,128)(2,1)}, bf16[32,56,128]{2,1,0:T(8,128)(2,1)S(1)}) custom-call(s32[4]{0:T(128)S(1)} %pad_add_fusion.place_ref, bf16[32,32,400]{2,1,0:T(8,128)(2,1)S(1)} %copy-done), custom_call_target="tpu_custom_call" | custom-call | tf_op jit(solution)/shard_map/prep/pallas_call | solution.py:63
  4.7 8.6 %all-to-all-start = ((bf16[32,112,128]{2,1,0:T(8,128)(2,1)}), bf16[32,112,128]{2,1,0:T(8,128)(2,1)S(1)}, u32[]{:S(2)}, u32[]{:S(2)}) async-start(bf16[32,112,128]{2,1,0:T(8,128)(2,1)} %get-tuple-element.7), calls=%async_computation | async-start | bytes 1835008 | tf_op jit(solution)/shard_map/all_to_all | solution.py:183
  13.3 7.0 %collective-permute-start = (bf16[32,56,128]{2,1,0:T(8,128)(2,1)S(1)}, bf16[32,56,128]{2,1,0:T(8,128)(2,1)}, u32[]{:S(2)}, u32[]{:S(2)}) collective-permute-start(bf16[32,56,128]{2,1,0:T(8,128)(2,1)S(1)} %get-tuple-element.8), channel_id=1, source_target_pairs={{0,1},{1,0},{2,3},{3,2},{4,5},{5,4},{6,7},{7,6},{8,9},{9,8},{10,11... | collective-permute-start | bytes 1376264 | tf_op jit(solution)/shard_map/ppermute | solution.py:191
  20.3 0.6 fusion.5
  25.8 7.4 %collective-permute-done = bf16[32,56,128]{2,1,0:T(8,128)(2,1)} collective-permute-done((bf16[32,56,128]{2,1,0:T(8,128)(2,1)S(1)}, bf16[32,56,128]{2,1,0:T(8,128)(2,1)}, u32[]{:S(2)}, u32[]{:S(2)}) %collective-permute-start) | collective-permute-done | bytes 458784 | tf_op jit(solution)/shard_map/ppermute | solution.py:191
  33.2 0.0 all-to-all-done.own_ref
  33.2 7.9 %all-to-all-start.1 = ((bf16[32,56,128]{2,1,0:T(8,128)(2,1)}), bf16[32,56,128]{2,1,0:T(8,128)(2,1)S(1)}, u32[]{:S(2)}, u32[]{:S(2)}) async-start(bf16[32,56,128]{2,1,0:T(8,128)(2,1)} %collective-permute-done), calls=%async_computation.1 | async-start | bytes 917504 | tf_op jit(solution)/shard_map/all_to_all | solution.py:183
  41.2 8.5 %collective-permute-start.1 = (bf16[2,112,128]{2,1,0:T(8,128)(2,1)S(1)}, bf16[2,112,128]{2,1,0:T(8,128)(2,1)S(1)}, u32[]{:S(2)}, u32[]{:S(2)}) collective-permute-start(bf16[2,112,128]{2,1,0:T(8,128)(2,1)S(1)} %pad_maximum_fusion.1), channel_id=1, source_target_pairs={{0,64},{64,128},{128,192},{192,1},{1,65},{65,129},{129,193},{193,0... | collective-permute-start | bytes 172040 | tf_op jit(solution)/shard_map/ppermute | solution.py:179
  49.6 2.3 %collective-permute-start.2 = (bf16[2,112,128]{2,1,0:T(8,128)(2,1)S(1)}, bf16[2,112,128]{2,1,0:T(8,128)(2,1)S(1)}, u32[]{:S(2)}, u32[]{:S(2)}) collective-permute-start(bf16[2,112,128]{2,1,0:T(8,128)(2,1)S(1)} %pad_maximum_fusion.1), channel_id=1, source_target_pairs={{0,193},{64,0},{128,64},{192,128},{1,192},{65,1},{129,65},{193,129... | collective-permute-start | bytes 172040 | tf_op jit(solution)/shard_map/ppermute | solution.py:179
  51.9 2.1 %collective-permute-done.1 = bf16[2,112,128]{2,1,0:T(8,128)(2,1)S(1)} collective-permute-done((bf16[2,112,128]{2,1,0:T(8,128)(2,1)S(1)}, bf16[2,112,128]{2,1,0:T(8,128)(2,1)S(1)}, u32[]{:S(2)}, u32[]{:S(2)}) %collective-permute-start.1) | collective-permute-done | bytes 57376 | tf_op jit(solution)/shard_map/ppermute | solution.py:179
  54.0 0.0 collective-permute-done.2
  54.0 4.3 %collective-permute-start.3 = (bf16[2,112,128]{2,1,0:T(8,128)(2,1)S(1)}, bf16[2,112,128]{2,1,0:T(8,128)(2,1)S(1)}, u32[]{:S(2)}, u32[]{:S(2)}) collective-permute-start(bf16[2,112,128]{2,1,0:T(8,128)(2,1)S(1)} %add_add_fusion.near_ref), channel_id=1, source_target_pairs={{0,192},{64,1},{128,65},{192,129},{1,193},{65,0},{129,64},{193,128... | collective-permute-start | bytes 172040 | tf_op jit(solution)/shard_map/ppermute | solution.py:179
  58.3 0.2 collective-permute-start.4
  58.6 0.0 all-to-all-done.1.other_ref
  58.6 1.7 %collective-permute-done.3.below_ref = bf16[2,112,128]{2,1,0:T(8,128)(2,1)S(1)} collective-permute-done((bf16[2,112,128]{2,1,0:T(8,128)(2,1)S(1)}, bf16[2,112,128]{2,1,0:T(8,128)(2,1)S(1)}, u32[]{:S(2)}, u32[]{:S(2)}) %collective-permute-start.3) | collective-permute-done | bytes 57376 | tf_op jit(solution)/shard_map/ppermute | solution.py:179
  60.2 2.9 %collective-permute-done.4.above_ref = bf16[2,112,128]{2,1,0:T(8,128)(2,1)S(1)} collective-permute-done((bf16[2,112,128]{2,1,0:T(8,128)(2,1)S(1)}, bf16[2,112,128]{2,1,0:T(8,128)(2,1)S(1)}, u32[]{:S(2)}, u32[]{:S(2)}) %collective-permute-start.4) | collective-permute-done | bytes 57376 | tf_op jit(solution)/shard_map/ppermute | solution.py:179
  63.2 2.3 %cross.1 = bf16[32,112,128]{2,1,0:T(8,128)(2,1)} custom-call(s32[4]{0:T(128)S(1)} %pad_add_fusion.place_ref, bf16[32,112,128]{2,1,0:T(8,128)(2,1)S(1)} %all-to-all-done.own_ref, bf16[32,56,128]{2,1,0:T(8,128)(2,1)S(1)} %all-to-all-done.1.other_ref, bf16[2,112,128]{2,1,0:T(8,128)(2,1)S(1)} %add_add_fusion.near_ref, ...), custom_call_target="tpu_custom_call" | custom-call | tf_op jit(solution)/shard_map/cross/pallas_call | solution.py:140
  65.4 11.0 %all-to-all-start.2 = ((bf16[32,112,128]{2,1,0:T(8,128)(2,1)}), bf16[32,112,128]{2,1,0:T(8,128)(2,1)S(1)}, u32[]{:S(2)}, u32[]{:S(2)}) async-start(bf16[32,112,128]{2,1,0:T(8,128)(2,1)} %cross.1), calls=%async_computation.2 | async-start | bytes 1835008 | tf_op jit(solution)/shard_map/all_to_all | solution.py:183
  76.5 1.8 %cosine_convert_fusion = (bf16[1,200,400]{2,1,0:T(8,128)(2,1)S(1)}, bf16[1,200,400]{2,1,0:T(8,128)(2,1)S(1)}) fusion(s32[400]{0:T(512)S(1)} %iota_add_fusion), kind=kLoop, calls=%fused_computation.5 | loop fusion | flops 960000 | bytes 321600 | tf_op jit(solution)/shard_map/convert
  78.2 0.1 pad_maximum_fusion.refs_1_
  78.3 13.6 %all-to-all-done.2.refs_0_ = bf16[32,112,128]{2,1,0:T(8,128)(2,1)S(1)} async-done(((bf16[32,112,128]{2,1,0:T(8,128)(2,1)}), bf16[32,112,128]{2,1,0:T(8,128)(2,1)S(1)}, u32[]{:S(2)}, u32[]{:S(2)}) %all-to-all-start.2) | async-done | bytes 917536 | tf_op jit(solution)/shard_map/all_to_all | solution.py:183
  91.9 2.6 %lag.1 = bf16[2,16,32,400]{3,2,1,0:T(8,128)(2,1)} custom-call(bf16[32,112,128]{2,1,0:T(8,128)(2,1)S(1)} %all-to-all-done.2.refs_0_, bf16[2,200,400]{2,1,0:T(8,128)(2,1)S(1)} %pad_maximum_fusion.refs_1_), custom_call_target="tpu_custom_call" | custom-call | tf_op jit(solution)/shard_map/lag/pallas_call | solution.py:165
  (4 shorter events, 0.0 us)
Async XLA Ops:
  0.0 0.7 copy-start.1
  0.7 1.2 %copy-start = (bf16[32,32,400]{2,1,0:T(8,128)(2,1)S(1)}, bf16[32,32,400]{2,1,0:T(8,128)(2,1)}, u32[]{:S(2)}) copy-start(bf16[32,32,400]{2,1,0:T(8,128)(2,1)} %spectra_ref.1) | copy-start | bytes 2457604
  4.7 28.5 %all-to-all-start = ((bf16[32,112,128]{2,1,0:T(8,128)(2,1)}), bf16[32,112,128]{2,1,0:T(8,128)(2,1)S(1)}, u32[]{:S(2)}, u32[]{:S(2)}) async-start(bf16[32,112,128]{2,1,0:T(8,128)(2,1)} %get-tuple-element.7), calls=%async_computation | async-start | bytes 1835008 | tf_op jit(solution)/shard_map/all_to_all | solution.py:183
  13.3 19.9 %collective-permute-start = (bf16[32,56,128]{2,1,0:T(8,128)(2,1)S(1)}, bf16[32,56,128]{2,1,0:T(8,128)(2,1)}, u32[]{:S(2)}, u32[]{:S(2)}) collective-permute-start(bf16[32,56,128]{2,1,0:T(8,128)(2,1)S(1)} %get-tuple-element.8), channel_id=1, source_target_pairs={{0,1},{1,0},{2,3},{3,2},{4,5},{5,4},{6,7},{7,6},{8,9},{9,8},{10,11... | collective-permute-start | bytes 1376264 | tf_op jit(solution)/shard_map/ppermute | solution.py:191
  33.2 25.4 %all-to-all-start.1 = ((bf16[32,56,128]{2,1,0:T(8,128)(2,1)}), bf16[32,56,128]{2,1,0:T(8,128)(2,1)S(1)}, u32[]{:S(2)}, u32[]{:S(2)}) async-start(bf16[32,56,128]{2,1,0:T(8,128)(2,1)} %collective-permute-done), calls=%async_computation.1 | async-start | bytes 917504 | tf_op jit(solution)/shard_map/all_to_all | solution.py:183
  41.2 12.8 %collective-permute-start.1 = (bf16[2,112,128]{2,1,0:T(8,128)(2,1)S(1)}, bf16[2,112,128]{2,1,0:T(8,128)(2,1)S(1)}, u32[]{:S(2)}, u32[]{:S(2)}) collective-permute-start(bf16[2,112,128]{2,1,0:T(8,128)(2,1)S(1)} %pad_maximum_fusion.1), channel_id=1, source_target_pairs={{0,64},{64,128},{128,192},{192,1},{1,65},{65,129},{129,193},{193,0... | collective-permute-start | bytes 172040 | tf_op jit(solution)/shard_map/ppermute | solution.py:179
  49.6 4.4 %collective-permute-start.2 = (bf16[2,112,128]{2,1,0:T(8,128)(2,1)S(1)}, bf16[2,112,128]{2,1,0:T(8,128)(2,1)S(1)}, u32[]{:S(2)}, u32[]{:S(2)}) collective-permute-start(bf16[2,112,128]{2,1,0:T(8,128)(2,1)S(1)} %pad_maximum_fusion.1), channel_id=1, source_target_pairs={{0,193},{64,0},{128,64},{192,128},{1,192},{65,1},{129,65},{193,129... | collective-permute-start | bytes 172040 | tf_op jit(solution)/shard_map/ppermute | solution.py:179
  54.0 6.2 %collective-permute-start.3 = (bf16[2,112,128]{2,1,0:T(8,128)(2,1)S(1)}, bf16[2,112,128]{2,1,0:T(8,128)(2,1)S(1)}, u32[]{:S(2)}, u32[]{:S(2)}) collective-permute-start(bf16[2,112,128]{2,1,0:T(8,128)(2,1)S(1)} %add_add_fusion.near_ref), channel_id=1, source_target_pairs={{0,192},{64,1},{128,65},{192,129},{1,193},{65,0},{129,64},{193,128... | collective-permute-start | bytes 172040 | tf_op jit(solution)/shard_map/ppermute | solution.py:179
  58.3 4.8 %collective-permute-start.4 = (bf16[2,112,128]{2,1,0:T(8,128)(2,1)S(1)}, bf16[2,112,128]{2,1,0:T(8,128)(2,1)S(1)}, u32[]{:S(2)}, u32[]{:S(2)}) collective-permute-start(bf16[2,112,128]{2,1,0:T(8,128)(2,1)S(1)} %add_add_fusion.near_ref), channel_id=1, source_target_pairs={{0,65},{64,129},{128,193},{192,0},{1,64},{65,128},{129,192},{193,1... | collective-permute-start | bytes 172040 | tf_op jit(solution)/shard_map/ppermute | solution.py:179
  65.4 26.5 %all-to-all-start.2 = ((bf16[32,112,128]{2,1,0:T(8,128)(2,1)}), bf16[32,112,128]{2,1,0:T(8,128)(2,1)S(1)}, u32[]{:S(2)}, u32[]{:S(2)}) async-start(bf16[32,112,128]{2,1,0:T(8,128)(2,1)} %cross.1), calls=%async_computation.2 | async-start | bytes 1835008 | tf_op jit(solution)/shard_map/all_to_all | solution.py:183

commit v3 on v2

--- a/solution.py
+++ b/solution.py
@@ -29,17 +29,29 @@
     return jnp.stack([jnp.cos(angle), -jnp.sin(angle)], axis=0).astype(jnp.bfloat16)
 
 
-def prep_kernel(place_ref, spectra_ref, out_ref, theirs_ref, rows_ref):
-    day = place_ref[0]
+def prep_kernel(spectra_ref, out_ref, theirs_ref, held_ref, sems, rows_ref):
+    day = lax.axis_index("day")
+    copies = []
+    for which in range(2):
+        half = (day + which) % 2
+        copies.append(
+            pltpu.make_async_copy(
+                spectra_ref.at[pl.ds(half * 16, 16)],
+                held_ref.at[pl.ds(which * 16, 16)],
+                sems.at[which],
+            )
+        )
+    for copy in copies:
+        copy.start()
     low = lax.broadcasted_iota(jnp.int32, (BINS, 128), 1) < 64
-    pad = SIDE * SHARE - BINS
-    rows_ref[BINS * 16 :, :] = jnp.zeros((pad * 16, 128), jnp.float32)
-    for half in range(2):
+    rows_ref[BINS * 16 :, :] = jnp.zeros(((SIDE * SHARE - BINS) * 16, 128), jnp.float32)
+    for which in range(2):
+        copies[which].wait()
         for pair in range(4):
             parts = []
             for a in (2 * pair, 2 * pair + 1):
                 for q in range(2):
-                    parts.append(spectra_ref[half * 16 + q * 8 + a].astype(jnp.float32))
+                    parts.append(held_ref[which * 16 + q * 8 + a].astype(jnp.float32))
             turned = jnp.concatenate(parts, axis=0).T
             re, im = turned[:BINS], turned[BINS:]
             power = re * re + im * im
@@ -48,33 +60,40 @@
             re, im = re * factor, im * factor
             first = jnp.where(low, re, pltpu.roll(im, 64, 1))
             second = jnp.where(low, pltpu.roll(re, 64, 1), im)
-            at = half * 8 + 2 * pair
+            at = which * 8 + 2 * pair
             rows_ref[pl.ds(at, BINS, stride=16), :] = first
             rows_ref[pl.ds(at + 1, BINS, stride=16), :] = second
     for dest in range(SIDE):
         chunk = rows_ref[dest * ROWS : (dest + 1) * ROWS, :]
         out_ref[dest] = chunk.astype(jnp.bfloat16)
-        split = chunk.reshape(SHARE, 2, 8, 128)
-        theirs = jnp.where(day == 0, split[:, 1], split[:, 0])
-        theirs_ref[dest] = theirs.reshape(HALF, 128).astype(jnp.bfloat16)
-
-
-def prep(place, spectra):
+        theirs = chunk.reshape(SHARE, 2, 8, 128)[:, 1].reshape(HALF, 128)
+        count = min(HALF, BINS * 8 - dest * HALF)
+        if count > 0:
+            theirs_ref[dest * HALF : dest * HALF + count, :] = theirs[:count].astype(jnp.bfloat16)
+
+
+def prep(spectra):
     return pl.pallas_call(
         prep_kernel,
         out_shape=(
             jax.ShapeDtypeStruct((SIDE, ROWS, 128), jnp.bfloat16),
-            jax.ShapeDtypeStruct((SIDE, HALF, 128), jnp.bfloat16),
+            jax.ShapeDtypeStruct((BINS * 8, 128), jnp.bfloat16),
         ),
-        in_specs=[SMEM, VMEM],
+        in_specs=[pl.BlockSpec(memory_space=pl.ANY)],
         out_specs=(VMEM, VMEM),
-        scratch_shapes=[pltpu.VMEM((SIDE * ROWS, 128), jnp.float32)],
-        compiler_params=ROOM,
+        scratch_shapes=[
+            pltpu.VMEM(spectra.shape, jnp.bfloat16),
+            pltpu.SemaphoreType.DMA((2,)),
+            pltpu.VMEM((SIDE * ROWS, 128), jnp.float32),
+        ],
+        compiler_params=pltpu.CompilerParams(vmem_limit_bytes=60 * 1024 * 1024),
         name="prep",
-    )(place, spectra)
-
-
-def weights(value):
+    )(spectra)
+
+
+def weights(value, day_of):
+    swapped = jnp.concatenate([value[8:], value[:8]], axis=0)
+    value = jnp.where(day_of == 0, value, swapped)
     lane = lax.broadcasted_iota(jnp.int32, value.shape, 1)
     odd = (lane // 32) % 2 == 1
     zero = jnp.zeros_like(value)
@@ -96,14 +115,14 @@
     return rows
 
 
-def cross_kernel(place_ref, own_ref, other_ref, near_ref, below_ref, above_ref, out_ref):
-    day, z_lo = place_ref[0], place_ref[1]
+def cross_kernel(owners_ref, own_ref, other_ref, near_ref, below_ref, above_ref, out_ref):
+    day, z_lo = lax.axis_index("day"), lax.axis_index("z")
     blocks = []
     for which in range(2):
         day_of = (day + which) % 2
         chosen = []
         for step in range(STEPS):
-            home = place_ref[2 + step] // SIDE + 4 * day_of
+            home = owners_ref[step] // SIDE + 4 * day_of
             delta = (day * 4 + z_lo - home + 16) % 8
             use_near = (delta == 7) | (delta <= 1)
             use_below = delta <= 4
@@ -117,14 +136,17 @@
     for k in range(SHARE):
         sides = []
         for which in range(2):
-            parts = [weights(blocks[which][step][k * 16 : k * 16 + 16]) for step in range(STEPS)]
+            day_of = (day + which) % 2
+            parts = [
+                weights(blocks[which][step][k * 16 : k * 16 + 16], day_of) for step in range(STEPS)
+            ]
             order = []
             for at in range(4):
                 for step in range(STEPS):
                     order.append(parts[step][at])
             sides.append(jnp.concatenate(order, axis=0))
         right = jnp.concatenate(sides, axis=1).astype(jnp.bfloat16)
-        own = jnp.where(day == 0, own_all[:, k, 0], own_all[:, k, 1]).reshape(SIDE * 8, 128)
+        own = own_all[:, k, 0].reshape(SIDE * 8, 128)
         other = other_all[:, k].reshape(SIDE * 8, 128)
         left = jnp.concatenate([own, other], axis=1).astype(jnp.bfloat16)
         product = lax.dot_general(
@@ -136,7 +158,7 @@
         out_ref[:, k * 16 : k * 16 + 16, :] = both.astype(jnp.bfloat16)
 
 
-def cross(place, own, other, near, below, above):
+def cross(owners, own, other, near, below, above):
     return pl.pallas_call(
         cross_kernel,
         out_shape=jax.ShapeDtypeStruct((SIDE, ROWS, 128), jnp.bfloat16),
@@ -144,7 +166,7 @@
         out_specs=VMEM,
         compiler_params=ROOM,
         name="cross",
-    )(place, own, other, near, below, above)
+    )(owners, own, other, near, below, above)
 
 
 def lag_kernel(norm, summed_ref, table_ref, out_ref, rows_ref):
@@ -184,10 +206,8 @@
 
 
 def local(spectra, owners):
-    day = lax.axis_index("day").astype(jnp.int32)
-    z_lo = lax.axis_index("z").astype(jnp.int32)
-    place = jnp.concatenate([jnp.stack([day, z_lo]), owners])
-    mine, theirs = prep(place, spectra)
+    z_lo = lax.axis_index("z")
+    mine, theirs = prep(spectra)
     arrived = lax.ppermute(theirs, "day", [(0, 1), (1, 0)])
     own = spread(mine)
     pieces = []
@@ -197,8 +217,10 @@
     held = jnp.stack(pieces)
     near = held + hop(held, 1) + hop(held, -1)
     below, above = hop(near, 3), hop(near, -3)
+    arrived = jnp.pad(arrived, ((0, SIDE * HALF - BINS * 8), (0, 0))).reshape(SIDE, HALF, 128)
+    arrived, near = lax.optimization_barrier((arrived, near))
     other = spread(arrived)
-    home = spread(cross(place, own, other, near, below, above))
+    home = spread(cross(owners, own, other, near, below, above))
     norm = 1.0 / math.sqrt(2 * spectra.shape[1] * BINS)
     return lag(norm, home, lag_table())
 

time: 95 us -> 87.8 us (0.924)
  the two profiles are of different devices: /device:TPU:1 before, /device:TPU:33 now
where the time goes in v3:
time: 87.8 us; the launch traced here: 87.3 us
  starting transfers between devices  39 us (44%)
  waiting for transfers between devices  31.8 us (36%)
  Pallas kernels  8.41 us (10%)
  between operations  4.88 us (6%)
  other arithmetic  1.84 us (2%)
  local copies, waits for them, and re-layouts  1.36 us (2%)
    all_to_all x3, starting transfers between devices, spread(): return lax.all_to_all(array, PLANE, 0, 0, tiled=True)  26.2 us
    all_to_all x3, waiting for transfers between devices, spread(): return lax.all_to_all(array, PLANE, 0, 0, tiled=True)  18.1 us
    ppermute x1, waiting for transfers between devices, local(): arrived = lax.ppermute(theirs, 'day', [(0, 1), (1, 0)])  7.26 us
    ppermute x4, starting transfers between devices, hop(): return lax.ppermute(array, ('z', 'day'), ring)  6.69 us
    ppermute x4, waiting for transfers between devices, hop(): return lax.ppermute(array, ('z', 'day'), ring)  6.41 us
    ppermute x1, starting transfers between devices, local(): arrived = lax.ppermute(theirs, 'day', [(0, 1), (1, 0)])  6.1 us
    pallas_call x1, Pallas kernels, prep(): pl.pallas_call(prep_kernel, out_shape=(jax.ShapeDtypeStruct((SIDE, ROWS,...  3.39 us
    pallas_call x1, Pallas kernels, lag(): pl.pallas_call(kernel, out_shape=jax.ShapeDtypeStruct((STEPS, 16, 32, LAG...  2.7 us
  transfers between devices with their start and end apart: 8, of which 8 were waited for; matrix products, arithmetic and copies ran while one was open for 4% of the time, Pallas kernels for 0%

profile of v3, /device:TPU:33, one launch (start us, length us, event | category | flops | bytes accessed | tf_op | source)
XLA Modules:
  0.0 87.3 jit_solution(16840546392928140350)
XLA Ops:
  0.0 3.4 %prep.1 = (bf16[32,112,128]{2,1,0:T(8,128)(2,1)}, bf16[1600,128]{1,0:T(8,128)(2,1)}) custom-call(bf16[32,32,400]{2,1,0:T(8,128)(2,1)} %spectra_ref.1), custom_call_target="tpu_custom_call" | custom-call | tf_op jit(solution)/shard_map/prep/pallas_call | solution.py:76
  3.4 0.0 copy-start.1
  3.4 7.9 %all-to-all-start = ((bf16[32,112,128]{2,1,0:T(8,128)(2,1)}), bf16[32,112,128]{2,1,0:T(8,128)(2,1)S(1)}, u32[]{:S(2)}, u32[]{:S(2)}) async-start(bf16[32,112,128]{2,1,0:T(8,128)(2,1)} %get-tuple-element.9), calls=%async_computation | async-start | bytes 1835008 | tf_op jit(solution)/shard_map/all_to_all | solution.py:205
  11.3 0.0 copy-start
  11.3 0.0 copy-done.1
  11.3 6.1 %collective-permute-start = (bf16[1600,128]{1,0:T(8,128)(2,1)S(1)}, bf16[1600,128]{1,0:T(8,128)(2,1)S(1)}, u32[]{:S(2)}, u32[]{:S(2)}) collective-permute-start(bf16[1600,128]{1,0:T(8,128)(2,1)S(1)} %copy-done.1), channel_id=1, source_target_pairs={{0,1},{1,0},{2,3},{3,2},{4,5},{5,4},{6,7},{7,6},{8,9},{9,8},{10,11... | collective-permute-start | bytes 1228808 | tf_op jit(solution)/shard_map/ppermute | solution.py:211
  17.4 0.0 copy-done
  17.4 0.6 fusion.5
  22.8 4.1 %all-to-all-done.own_ref = bf16[32,112,128]{2,1,0:T(8,128)(2,1)S(1)} async-done(((bf16[32,112,128]{2,1,0:T(8,128)(2,1)}), bf16[32,112,128]{2,1,0:T(8,128)(2,1)S(1)}, u32[]{:S(2)}, u32[]{:S(2)}) %all-to-all-start) | async-done | bytes 917536 | tf_op jit(solution)/shard_map/all_to_all | solution.py:205
  26.9 1.7 %collective-permute-start.1 = (bf16[2,112,128]{2,1,0:T(8,128)(2,1)S(1)}, bf16[2,112,128]{2,1,0:T(8,128)(2,1)S(1)}, u32[]{:S(2)}, u32[]{:S(2)}) collective-permute-start(bf16[2,112,128]{2,1,0:T(8,128)(2,1)S(1)} %pad_maximum_fusion.1), channel_id=1, source_target_pairs={{0,64},{64,128},{128,192},{192,1},{1,65},{65,129},{129,193},{193,0... | collective-permute-start | bytes 172040 | tf_op jit(solution)/shard_map/ppermute | solution.py:201
  28.6 0.0 collective-permute-start.2
  28.6 7.3 %collective-permute-done = bf16[1600,128]{1,0:T(8,128)(2,1)S(1)} collective-permute-done((bf16[1600,128]{1,0:T(8,128)(2,1)S(1)}, bf16[1600,128]{1,0:T(8,128)(2,1)S(1)}, u32[]{:S(2)}, u32[]{:S(2)}) %collective-permute-start) | collective-permute-done | bytes 409632 | tf_op jit(solution)/shard_map/ppermute | solution.py:211
  35.9 0.8 pad.4
  36.7 0.5 collective-permute-done.1
  37.2 0.3 collective-permute-done.2
  37.5 7.5 %all-to-all-start.1 = ((bf16[32,56,128]{2,1,0:T(8,128)(2,1)}), bf16[32,56,128]{2,1,0:T(8,128)(2,1)S(1)}, u32[]{:S(2)}, u32[]{:S(2)}) async-start(bf16[32,56,128]{2,1,0:T(8,128)(2,1)} %bitcast), calls=%async_computation.1 | async-start | bytes 917504 | tf_op jit(solution)/shard_map/all_to_all | solution.py:205
  45.0 4.6 %collective-permute-start.3 = (bf16[2,112,128]{2,1,0:T(8,128)(2,1)S(1)}, bf16[2,112,128]{2,1,0:T(8,128)(2,1)S(1)}, u32[]{:S(2)}, u32[]{:S(2)}) collective-permute-start(bf16[2,112,128]{2,1,0:T(8,128)(2,1)S(1)} %add_add_fusion.near_ref), channel_id=1, source_target_pairs={{0,192},{64,1},{128,65},{192,129},{1,193},{65,0},{129,64},{193,128... | collective-permute-start | bytes 172040 | tf_op jit(solution)/shard_map/ppermute | solution.py:201
  49.6 0.4 collective-permute-start.4
  50.0 4.6 %collective-permute-done.3.below_ref = bf16[2,112,128]{2,1,0:T(8,128)(2,1)S(1)} collective-permute-done((bf16[2,112,128]{2,1,0:T(8,128)(2,1)S(1)}, bf16[2,112,128]{2,1,0:T(8,128)(2,1)S(1)}, u32[]{:S(2)}, u32[]{:S(2)}) %collective-permute-start.3) | collective-permute-done | bytes 57376 | tf_op jit(solution)/shard_map/ppermute | solution.py:201
  54.6 1.1 %collective-permute-done.4.above_ref = bf16[2,112,128]{2,1,0:T(8,128)(2,1)S(1)} collective-permute-done((bf16[2,112,128]{2,1,0:T(8,128)(2,1)S(1)}, bf16[2,112,128]{2,1,0:T(8,128)(2,1)S(1)}, u32[]{:S(2)}, u32[]{:S(2)}) %collective-permute-start.4) | collective-permute-done | bytes 57376 | tf_op jit(solution)/shard_map/ppermute | solution.py:201
  55.6 0.4 all-to-all-done.1.other_ref
  56.0 2.3 %cross.1 = bf16[32,112,128]{2,1,0:T(8,128)(2,1)} custom-call(s32[2]{0:T(128)S(1)} %copy-done, bf16[32,112,128]{2,1,0:T(8,128)(2,1)S(1)} %all-to-all-done.own_ref, bf16[32,56,128]{2,1,0:T(8,128)(2,1)S(1)} %all-to-all-done.1.other_ref, bf16[2,112,128]{2,1,0:T(8,128)(2,1)S(1)} %add_add_fusion.near_ref, ...), custom_call_target="tpu_custom_call" | custom-call | tf_op jit(solution)/shard_map/cross/pallas_call | solution.py:162
  58.3 10.8 %all-to-all-start.2 = ((bf16[32,112,128]{2,1,0:T(8,128)(2,1)}), bf16[32,112,128]{2,1,0:T(8,128)(2,1)S(1)}, u32[]{:S(2)}, u32[]{:S(2)}) async-start(bf16[32,112,128]{2,1,0:T(8,128)(2,1)} %cross.1), calls=%async_computation.2 | async-start | bytes 1835008 | tf_op jit(solution)/shard_map/all_to_all | solution.py:205
  69.2 1.8 %cosine_convert_fusion = (bf16[1,200,400]{2,1,0:T(8,128)(2,1)S(1)}, bf16[1,200,400]{2,1,0:T(8,128)(2,1)S(1)}) fusion(s32[400]{0:T(512)S(1)} %iota_add_fusion), kind=kLoop, calls=%fused_computation.5 | loop fusion | flops 960000 | bytes 321600 | tf_op jit(solution)/shard_map/convert
  70.9 0.1 pad_maximum_fusion.refs_1_
  71.0 13.6 %all-to-all-done.2.refs_0_ = bf16[32,112,128]{2,1,0:T(8,128)(2,1)S(1)} async-done(((bf16[32,112,128]{2,1,0:T(8,128)(2,1)}), bf16[32,112,128]{2,1,0:T(8,128)(2,1)S(1)}, u32[]{:S(2)}, u32[]{:S(2)}) %all-to-all-start.2) | async-done | bytes 917536 | tf_op jit(solution)/shard_map/all_to_all | solution.py:205
  84.6 2.7 %lag.1 = bf16[2,16,32,400]{3,2,1,0:T(8,128)(2,1)} custom-call(bf16[32,112,128]{2,1,0:T(8,128)(2,1)S(1)} %all-to-all-done.2.refs_0_, bf16[2,200,400]{2,1,0:T(8,128)(2,1)S(1)} %pad_maximum_fusion.refs_1_), custom_call_target="tpu_custom_call" | custom-call | tf_op jit(solution)/shard_map/lag/pallas_call | solution.py:187
  (4 shorter events, 0.0 us)
Async XLA Ops:
  3.4 7.9 %copy-start.1 = (bf16[1600,128]{1,0:T(8,128)(2,1)S(1)}, bf16[1600,128]{1,0:T(8,128)(2,1)}, u32[]{:S(2)}) copy-start(bf16[1600,128]{1,0:T(8,128)(2,1)} %get-tuple-element.10) | copy-start | bytes 1228804
  3.4 23.5 %all-to-all-start = ((bf16[32,112,128]{2,1,0:T(8,128)(2,1)}), bf16[32,112,128]{2,1,0:T(8,128)(2,1)S(1)}, u32[]{:S(2)}, u32[]{:S(2)}) async-start(bf16[32,112,128]{2,1,0:T(8,128)(2,1)} %get-tuple-element.9), calls=%async_computation | async-start | bytes 1835008 | tf_op jit(solution)/shard_map/all_to_all | solution.py:205
  11.3 6.1 %copy-start = (s32[2]{0:T(128)S(1)}, s32[2]{0:T(128)}, u32[]{:S(2)}) copy-start(s32[2]{0:T(128)} %owners_ref.1) | copy-start | bytes 28
  11.3 24.6 %collective-permute-start = (bf16[1600,128]{1,0:T(8,128)(2,1)S(1)}, bf16[1600,128]{1,0:T(8,128)(2,1)S(1)}, u32[]{:S(2)}, u32[]{:S(2)}) collective-permute-start(bf16[1600,128]{1,0:T(8,128)(2,1)S(1)} %copy-done.1), channel_id=1, source_target_pairs={{0,1},{1,0},{2,3},{3,2},{4,5},{5,4},{6,7},{7,6},{8,9},{9,8},{10,11... | collective-permute-start | bytes 1228808 | tf_op jit(solution)/shard_map/ppermute | solution.py:211
  26.9 10.3 %collective-permute-start.1 = (bf16[2,112,128]{2,1,0:T(8,128)(2,1)S(1)}, bf16[2,112,128]{2,1,0:T(8,128)(2,1)S(1)}, u32[]{:S(2)}, u32[]{:S(2)}) collective-permute-start(bf16[2,112,128]{2,1,0:T(8,128)(2,1)S(1)} %pad_maximum_fusion.1), channel_id=1, source_target_pairs={{0,64},{64,128},{128,192},{192,1},{1,65},{65,129},{129,193},{193,0... | collective-permute-start | bytes 172040 | tf_op jit(solution)/shard_map/ppermute | solution.py:201
  28.6 8.9 %collective-permute-start.2 = (bf16[2,112,128]{2,1,0:T(8,128)(2,1)S(1)}, bf16[2,112,128]{2,1,0:T(8,128)(2,1)S(1)}, u32[]{:S(2)}, u32[]{:S(2)}) collective-permute-start(bf16[2,112,128]{2,1,0:T(8,128)(2,1)S(1)} %pad_maximum_fusion.1), channel_id=1, source_target_pairs={{0,193},{64,0},{128,64},{192,128},{1,192},{65,1},{129,65},{193,129... | collective-permute-start | bytes 172040 | tf_op jit(solution)/shard_map/ppermute | solution.py:201
  37.5 18.5 %all-to-all-start.1 = ((bf16[32,56,128]{2,1,0:T(8,128)(2,1)}), bf16[32,56,128]{2,1,0:T(8,128)(2,1)S(1)}, u32[]{:S(2)}, u32[]{:S(2)}) async-start(bf16[32,56,128]{2,1,0:T(8,128)(2,1)} %bitcast), calls=%async_computation.1 | async-start | bytes 917504 | tf_op jit(solution)/shard_map/all_to_all | solution.py:205
  45.0 9.5 %collective-permute-start.3 = (bf16[2,112,128]{2,1,0:T(8,128)(2,1)S(1)}, bf16[2,112,128]{2,1,0:T(8,128)(2,1)S(1)}, u32[]{:S(2)}, u32[]{:S(2)}) collective-permute-start(bf16[2,112,128]{2,1,0:T(8,128)(2,1)S(1)} %add_add_fusion.near_ref), channel_id=1, source_target_pairs={{0,192},{64,1},{128,65},{192,129},{1,193},{65,0},{129,64},{193,128... | collective-permute-start | bytes 172040 | tf_op jit(solution)/shard_map/ppermute | solution.py:201
  49.6 6.0 %collective-permute-start.4 = (bf16[2,112,128]{2,1,0:T(8,128)(2,1)S(1)}, bf16[2,112,128]{2,1,0:T(8,128)(2,1)S(1)}, u32[]{:S(2)}, u32[]{:S(2)}) collective-permute-start(bf16[2,112,128]{2,1,0:T(8,128)(2,1)S(1)} %add_add_fusion.near_ref), channel_id=1, source_target_pairs={{0,65},{64,129},{128,193},{192,0},{1,64},{65,128},{129,192},{193,1... | collective-permute-start | bytes 172040 | tf_op jit(solution)/shard_map/ppermute | solution.py:201
  58.3 26.3 %all-to-all-start.2 = ((bf16[32,112,128]{2,1,0:T(8,128)(2,1)}), bf16[32,112,128]{2,1,0:T(8,128)(2,1)S(1)}, u32[]{:S(2)}, u32[]{:S(2)}) async-start(bf16[32,112,128]{2,1,0:T(8,128)(2,1)} %cross.1), calls=%async_computation.2 | async-start | bytes 1835008 | tf_op jit(solution)/shard_map/all_to_all | solution.py:205

commit v4 on v3

--- a/solution.py
+++ b/solution.py
@@ -17,7 +17,6 @@
 ROWS = SHARE * 16
 HALF = SHARE * 8
 VMEM = pl.BlockSpec(memory_space=pltpu.VMEM)
-SMEM = pl.BlockSpec(memory_space=pltpu.SMEM)
 ROOM = pltpu.CompilerParams(vmem_limit_bytes=48 * 1024 * 1024)
 
 
@@ -115,22 +114,11 @@
     return rows
 
 
-def cross_kernel(owners_ref, own_ref, other_ref, near_ref, below_ref, above_ref, out_ref):
-    day, z_lo = lax.axis_index("day"), lax.axis_index("z")
-    blocks = []
-    for which in range(2):
-        day_of = (day + which) % 2
-        chosen = []
-        for step in range(STEPS):
-            home = owners_ref[step] // SIDE + 4 * day_of
-            delta = (day * 4 + z_lo - home + 16) % 8
-            use_near = (delta == 7) | (delta <= 1)
-            use_below = delta <= 4
-            near = near_ref[step].astype(jnp.float32)
-            below = below_ref[step].astype(jnp.float32)
-            above = above_ref[step].astype(jnp.float32)
-            chosen.append(jnp.where(use_near, near, jnp.where(use_below, below, above)))
-        blocks.append(chosen)
+def cross_kernel(own_ref, other_ref, mine_ref, away_ref, out_ref):
+    day = lax.axis_index("day")
+    blocks = [
+        [ref[step].astype(jnp.float32) for step in range(STEPS)] for ref in (mine_ref, away_ref)
+    ]
     own_all = own_ref[...].astype(jnp.float32).reshape(SIDE, SHARE, 2, 8, 128)
     other_all = other_ref[...].astype(jnp.float32).reshape(SIDE, SHARE, 8, 128)
     for k in range(SHARE):
@@ -158,15 +146,15 @@
         out_ref[:, k * 16 : k * 16 + 16, :] = both.astype(jnp.bfloat16)
 
 
-def cross(owners, own, other, near, below, above):
+def cross(own, other, mine, away):
     return pl.pallas_call(
         cross_kernel,
         out_shape=jax.ShapeDtypeStruct((SIDE, ROWS, 128), jnp.bfloat16),
-        in_specs=[SMEM] + [VMEM] * 5,
+        in_specs=[VMEM] * 4,
         out_specs=VMEM,
         compiler_params=ROOM,
         name="cross",
-    )(owners, own, other, near, below, above)
+    )(own, other, mine, away)
 
 
 def lag_kernel(norm, summed_ref, table_ref, out_ref, rows_ref):
@@ -195,10 +183,12 @@
     )(summed, table)
 
 
-def hop(array, shift):
-    at = [(r % 4) * 2 + r // 4 for r in range(8)]
-    ring = [(at[r], at[(r + shift) % 8]) for r in range(8)]
-    return lax.ppermute(array, ("z", "day"), ring)
+def line(array, shift):
+    return lax.ppermute(array, "z", [(at, (at + shift) % 4) for at in range(4)])
+
+
+def swap(array):
+    return lax.ppermute(array, "day", [(0, 1), (1, 0)])
 
 
 def spread(array):
@@ -208,19 +198,18 @@
 def local(spectra, owners):
     z_lo = lax.axis_index("z")
     mine, theirs = prep(spectra)
-    arrived = lax.ppermute(theirs, "day", [(0, 1), (1, 0)])
+    arrived = swap(theirs)
     own = spread(mine)
     pieces = []
     for step in range(STEPS):
         piece = lax.dynamic_index_in_dim(own, owners[step] % SIDE, 0, keepdims=False)
         pieces.append(jnp.where(owners[step] // SIDE == z_lo, piece, jnp.zeros_like(piece)))
     held = jnp.stack(pieces)
-    near = held + hop(held, 1) + hop(held, -1)
-    below, above = hop(near, 3), hop(near, -3)
+    block = held + line(held, 1) + line(held, 2) + line(held, 3)
     arrived = jnp.pad(arrived, ((0, SIDE * HALF - BINS * 8), (0, 0))).reshape(SIDE, HALF, 128)
-    arrived, near = lax.optimization_barrier((arrived, near))
+    arrived, block = lax.optimization_barrier((arrived, block))
     other = spread(arrived)
-    home = spread(cross(owners, own, other, near, below, above))
+    home = spread(cross(own, other, block, swap(block)))
     norm = 1.0 / math.sqrt(2 * spectra.shape[1] * BINS)
     return lag(norm, home, lag_table())
 

time: 87.8 us -> 86.3 us (0.983)
  the two profiles are of different devices: /device:TPU:33 before, /device:TPU:1 now
where the time goes in v4:
time: 86.3 us; the launch traced here: 85.9 us
  starting transfers between devices  36 us (42%)
  waiting for transfers between devices  34 us (39%)
  Pallas kernels  7.75 us (9%)
  between operations  4.88 us (6%)
  other arithmetic  1.85 us (2%)
  local copies, waits for them, and re-layouts  1.36 us (2%)
    all_to_all x3, starting transfers between devices, spread(): return lax.all_to_all(array, PLANE, 0, 0, tiled=True)  21.5 us
    all_to_all x3, waiting for transfers between devices, spread(): return lax.all_to_all(array, PLANE, 0, 0, tiled=True)  20.5 us
    ppermute x2, starting transfers between devices, swap(): return lax.ppermute(array, 'day', [(0, 1), (1, 0)])  9.08 us
    ppermute x3, waiting for transfers between devices, line(): return lax.ppermute(array, 'z', [(at, (at + shift) % 4) for at in range(4)])  8.25 us
    ppermute x3, starting transfers between devices, line(): return lax.ppermute(array, 'z', [(at, (at + shift) % 4) for at in range(4)])  5.43 us
    ppermute x2, waiting for transfers between devices, swap(): return lax.ppermute(array, 'day', [(0, 1), (1, 0)])  5.23 us
    pallas_call x1, Pallas kernels, prep(): pl.pallas_call(prep_kernel, out_shape=(jax.ShapeDtypeStruct((SIDE, ROWS,...  3.39 us
    pallas_call x1, Pallas kernels, lag(): pl.pallas_call(kernel, out_shape=jax.ShapeDtypeStruct((STEPS, 16, 32, LAG...  2.6 us
  transfers between devices with their start and end apart: 8, of which 6 were waited for; matrix products, arithmetic and copies ran while one was open for 4% of the time, Pallas kernels for 0%

profile of v4, /device:TPU:1, one launch (start us, length us, event | category | flops | bytes accessed | tf_op | source)
XLA Modules:
  0.0 85.9 jit_solution(4877033006410065522)
XLA Ops:
  0.0 3.4 %prep.1 = (bf16[32,112,128]{2,1,0:T(8,128)(2,1)}, bf16[1600,128]{1,0:T(8,128)(2,1)}) custom-call(bf16[32,32,400]{2,1,0:T(8,128)(2,1)} %spectra_ref.1), custom_call_target="tpu_custom_call" | custom-call | tf_op jit(solution)/shard_map/prep/pallas_call | solution.py:75
  3.4 0.0 copy-start.1
  3.4 8.7 %all-to-all-start = ((bf16[32,112,128]{2,1,0:T(8,128)(2,1)}), bf16[32,112,128]{2,1,0:T(8,128)(2,1)S(1)}, u32[]{:S(2)}, u32[]{:S(2)}) async-start(bf16[32,112,128]{2,1,0:T(8,128)(2,1)} %get-tuple-element.9), calls=%async_computation | async-start | bytes 1835008 | tf_op jit(solution)/shard_map/all_to_all | solution.py:195
  12.1 0.0 copy-start
  12.2 0.0 copy-done.1
  12.2 7.0 %collective-permute-start = (bf16[1600,128]{1,0:T(8,128)(2,1)S(1)}, bf16[1600,128]{1,0:T(8,128)(2,1)S(1)}, u32[]{:S(2)}, u32[]{:S(2)}) collective-permute-start(bf16[1600,128]{1,0:T(8,128)(2,1)S(1)} %copy-done.1), channel_id=1, source_target_pairs={{0,1},{1,0},{2,3},{3,2},{4,5},{5,4},{6,7},{7,6},{8,9},{9,8},{10,11... | collective-permute-start | bytes 1228808 | tf_op jit(solution)/shard_map/ppermute | solution.py:191
  19.2 0.0 copy-done
  19.2 0.6 fusion.5
  24.5 3.2 %all-to-all-done.own_ref = bf16[32,112,128]{2,1,0:T(8,128)(2,1)S(1)} async-done(((bf16[32,112,128]{2,1,0:T(8,128)(2,1)}), bf16[32,112,128]{2,1,0:T(8,128)(2,1)S(1)}, u32[]{:S(2)}, u32[]{:S(2)}) %all-to-all-start) | async-done | bytes 917536 | tf_op jit(solution)/shard_map/all_to_all | solution.py:195
  27.8 1.7 %collective-permute-start.1 = (bf16[2,112,128]{2,1,0:T(8,128)(2,1)S(1)}, bf16[2,112,128]{2,1,0:T(8,128)(2,1)S(1)}, u32[]{:S(2)}, u32[]{:S(2)}) collective-permute-start(bf16[2,112,128]{2,1,0:T(8,128)(2,1)S(1)} %pad_maximum_fusion.1), channel_id=1, source_target_pairs={{0,64},{64,128},{128,192},{192,0},{1,65},{65,129},{129,193},{193,1... | collective-permute-start | bytes 172040 | tf_op jit(solution)/shard_map/ppermute | solution.py:187
  29.5 3.0 %collective-permute-start.2 = (bf16[2,112,128]{2,1,0:T(8,128)(2,1)S(1)}, bf16[2,112,128]{2,1,0:T(8,128)(2,1)S(1)}, u32[]{:S(2)}, u32[]{:S(2)}) collective-permute-start(bf16[2,112,128]{2,1,0:T(8,128)(2,1)S(1)} %pad_maximum_fusion.1), channel_id=1, source_target_pairs={{0,128},{64,192},{128,0},{192,64},{1,129},{65,193},{129,1},{193,65... | collective-permute-start | bytes 172040 | tf_op jit(solution)/shard_map/ppermute | solution.py:187
  32.5 0.7 collective-permute-start.3
  33.2 0.0 collective-permute-done
  33.2 0.8 pad.4
  34.0 5.7 %collective-permute-done.1 = bf16[2,112,128]{2,1,0:T(8,128)(2,1)S(1)} collective-permute-done((bf16[2,112,128]{2,1,0:T(8,128)(2,1)S(1)}, bf16[2,112,128]{2,1,0:T(8,128)(2,1)S(1)}, u32[]{:S(2)}, u32[]{:S(2)}) %collective-permute-start.1) | collective-permute-done | bytes 57376 | tf_op jit(solution)/shard_map/ppermute | solution.py:187
  39.7 2.5 %collective-permute-done.2 = bf16[2,112,128]{2,1,0:T(8,128)(2,1)S(1)} collective-permute-done((bf16[2,112,128]{2,1,0:T(8,128)(2,1)S(1)}, bf16[2,112,128]{2,1,0:T(8,128)(2,1)S(1)}, u32[]{:S(2)}, u32[]{:S(2)}) %collective-permute-start.2) | collective-permute-done | bytes 57376 | tf_op jit(solution)/shard_map/ppermute | solution.py:187
  42.2 0.0 collective-permute-done.3
  42.3 7.6 %all-to-all-start.1 = ((bf16[32,56,128]{2,1,0:T(8,128)(2,1)}), bf16[32,56,128]{2,1,0:T(8,128)(2,1)S(1)}, u32[]{:S(2)}, u32[]{:S(2)}) async-start(bf16[32,56,128]{2,1,0:T(8,128)(2,1)} %bitcast), calls=%async_computation.1 | async-start | bytes 917504 | tf_op jit(solution)/shard_map/all_to_all | solution.py:195
  49.8 2.1 %collective-permute-start.4 = (bf16[2,112,128]{2,1,0:T(8,128)(2,1)S(1)}, bf16[2,112,128]{2,1,0:T(8,128)(2,1)S(1)}, u32[]{:S(2)}, u32[]{:S(2)}) collective-permute-start(bf16[2,112,128]{2,1,0:T(8,128)(2,1)S(1)} %add_add_fusion.mine_ref), channel_id=1, source_target_pairs={{0,1},{1,0},{2,3},{3,2},{4,5},{5,4},{6,7},{7,6},{8,9},{9,8},{10,11... | collective-permute-start | bytes 172040 | tf_op jit(solution)/shard_map/ppermute | solution.py:191
  51.9 5.2 %collective-permute-done.4.away_ref = bf16[2,112,128]{2,1,0:T(8,128)(2,1)S(1)} collective-permute-done((bf16[2,112,128]{2,1,0:T(8,128)(2,1)S(1)}, bf16[2,112,128]{2,1,0:T(8,128)(2,1)S(1)}, u32[]{:S(2)}, u32[]{:S(2)}) %collective-permute-start.4) | collective-permute-done | bytes 57376 | tf_op jit(solution)/shard_map/ppermute | solution.py:191
  57.2 3.6 %all-to-all-done.1.other_ref = bf16[32,56,128]{2,1,0:T(8,128)(2,1)S(1)} async-done(((bf16[32,56,128]{2,1,0:T(8,128)(2,1)}), bf16[32,56,128]{2,1,0:T(8,128)(2,1)S(1)}, u32[]{:S(2)}, u32[]{:S(2)}) %all-to-all-start.1) | async-done | bytes 458784 | tf_op jit(solution)/shard_map/all_to_all | solution.py:195
  60.8 1.8 %cross.1 = bf16[32,112,128]{2,1,0:T(8,128)(2,1)} custom-call(bf16[32,112,128]{2,1,0:T(8,128)(2,1)S(1)} %all-to-all-done.own_ref, bf16[32,56,128]{2,1,0:T(8,128)(2,1)S(1)} %all-to-all-done.1.other_ref, bf16[2,112,128]{2,1,0:T(8,128)(2,1)S(1)} %add_add_fusion.mine_ref, bf16[2,112,128]{2,1,0:T(8,128)(2,1)S(1)} %collective-permute-done.4.away_ref), custom_call_target="tpu_custom_call" | custom-call | tf_op jit(solution)/shard_map/cross/pallas_call | solution.py:150
  62.6 5.2 %all-to-all-start.2 = ((bf16[32,112,128]{2,1,0:T(8,128)(2,1)}), bf16[32,112,128]{2,1,0:T(8,128)(2,1)S(1)}, u32[]{:S(2)}, u32[]{:S(2)}) async-start(bf16[32,112,128]{2,1,0:T(8,128)(2,1)} %cross.1), calls=%async_computation.2 | async-start | bytes 1835008 | tf_op jit(solution)/shard_map/all_to_all | solution.py:195
  67.8 1.8 %cosine_convert_fusion = (bf16[1,200,400]{2,1,0:T(8,128)(2,1)S(1)}, bf16[1,200,400]{2,1,0:T(8,128)(2,1)S(1)}) fusion(s32[400]{0:T(512)S(1)} %iota_add_fusion), kind=kLoop, calls=%fused_computation.5 | loop fusion | flops 960000 | bytes 321600 | tf_op jit(solution)/shard_map/convert
  69.6 0.1 pad_maximum_fusion.refs_1_
  69.6 13.6 %all-to-all-done.2.refs_0_ = bf16[32,112,128]{2,1,0:T(8,128)(2,1)S(1)} async-done(((bf16[32,112,128]{2,1,0:T(8,128)(2,1)}), bf16[32,112,128]{2,1,0:T(8,128)(2,1)S(1)}, u32[]{:S(2)}, u32[]{:S(2)}) %all-to-all-start.2) | async-done | bytes 917536 | tf_op jit(solution)/shard_map/all_to_all | solution.py:195
  83.3 2.6 %lag.1 = bf16[2,16,32,400]{3,2,1,0:T(8,128)(2,1)} custom-call(bf16[32,112,128]{2,1,0:T(8,128)(2,1)S(1)} %all-to-all-done.2.refs_0_, bf16[2,200,400]{2,1,0:T(8,128)(2,1)S(1)} %pad_maximum_fusion.refs_1_), custom_call_target="tpu_custom_call" | custom-call | tf_op jit(solution)/shard_map/lag/pallas_call | solution.py:175
  (4 shorter events, 0.0 us)
Async XLA Ops:
  3.4 8.8 %copy-start.1 = (bf16[1600,128]{1,0:T(8,128)(2,1)S(1)}, bf16[1600,128]{1,0:T(8,128)(2,1)}, u32[]{:S(2)}) copy-start(bf16[1600,128]{1,0:T(8,128)(2,1)} %get-tuple-element.10) | copy-start | bytes 1228804
  3.4 24.3 %all-to-all-start = ((bf16[32,112,128]{2,1,0:T(8,128)(2,1)}), bf16[32,112,128]{2,1,0:T(8,128)(2,1)S(1)}, u32[]{:S(2)}, u32[]{:S(2)}) async-start(bf16[32,112,128]{2,1,0:T(8,128)(2,1)} %get-tuple-element.9), calls=%async_computation | async-start | bytes 1835008 | tf_op jit(solution)/shard_map/all_to_all | solution.py:195
  12.1 7.0 %copy-start = (s32[2]{0:T(128)S(1)}, s32[2]{0:T(128)}, u32[]{:S(2)}) copy-start(s32[2]{0:T(128)} %param.3) | copy-start | bytes 28
  12.2 21.0 %collective-permute-start = (bf16[1600,128]{1,0:T(8,128)(2,1)S(1)}, bf16[1600,128]{1,0:T(8,128)(2,1)S(1)}, u32[]{:S(2)}, u32[]{:S(2)}) collective-permute-start(bf16[1600,128]{1,0:T(8,128)(2,1)S(1)} %copy-done.1), channel_id=1, source_target_pairs={{0,1},{1,0},{2,3},{3,2},{4,5},{5,4},{6,7},{7,6},{8,9},{9,8},{10,11... | collective-permute-start | bytes 1228808 | tf_op jit(solution)/shard_map/ppermute | solution.py:191
  27.8 12.0 %collective-permute-start.1 = (bf16[2,112,128]{2,1,0:T(8,128)(2,1)S(1)}, bf16[2,112,128]{2,1,0:T(8,128)(2,1)S(1)}, u32[]{:S(2)}, u32[]{:S(2)}) collective-permute-start(bf16[2,112,128]{2,1,0:T(8,128)(2,1)S(1)} %pad_maximum_fusion.1), channel_id=1, source_target_pairs={{0,64},{64,128},{128,192},{192,0},{1,65},{65,129},{129,193},{193,1... | collective-permute-start | bytes 172040 | tf_op jit(solution)/shard_map/ppermute | solution.py:187
  29.5 12.8 %collective-permute-start.2 = (bf16[2,112,128]{2,1,0:T(8,128)(2,1)S(1)}, bf16[2,112,128]{2,1,0:T(8,128)(2,1)S(1)}, u32[]{:S(2)}, u32[]{:S(2)}) collective-permute-start(bf16[2,112,128]{2,1,0:T(8,128)(2,1)S(1)} %pad_maximum_fusion.1), channel_id=1, source_target_pairs={{0,128},{64,192},{128,0},{192,64},{1,129},{65,193},{129,1},{193,65... | collective-permute-start | bytes 172040 | tf_op jit(solution)/shard_map/ppermute | solution.py:187
  32.5 9.8 %collective-permute-start.3 = (bf16[2,112,128]{2,1,0:T(8,128)(2,1)S(1)}, bf16[2,112,128]{2,1,0:T(8,128)(2,1)S(1)}, u32[]{:S(2)}, u32[]{:S(2)}) collective-permute-start(bf16[2,112,128]{2,1,0:T(8,128)(2,1)S(1)} %pad_maximum_fusion.1), channel_id=1, source_target_pairs={{0,192},{64,0},{128,64},{192,128},{1,193},{65,1},{129,65},{193,129... | collective-permute-start | bytes 172040 | tf_op jit(solution)/shard_map/ppermute | solution.py:187
  42.3 18.5 %all-to-all-start.1 = ((bf16[32,56,128]{2,1,0:T(8,128)(2,1)}), bf16[32,56,128]{2,1,0:T(8,128)(2,1)S(1)}, u32[]{:S(2)}, u32[]{:S(2)}) async-start(bf16[32,56,128]{2,1,0:T(8,128)(2,1)} %bitcast), calls=%async_computation.1 | async-start | bytes 917504 | tf_op jit(solution)/shard_map/all_to_all | solution.py:195
  49.8 7.3 %collective-permute-start.4 = (bf16[2,112,128]{2,1,0:T(8,128)(2,1)S(1)}, bf16[2,112,128]{2,1,0:T(8,128)(2,1)S(1)}, u32[]{:S(2)}, u32[]{:S(2)}) collective-permute-start(bf16[2,112,128]{2,1,0:T(8,128)(2,1)S(1)} %add_add_fusion.mine_ref), channel_id=1, source_target_pairs={{0,1},{1,0},{2,3},{3,2},{4,5},{5,4},{6,7},{7,6},{8,9},{9,8},{10,11... | collective-permute-start | bytes 172040 | tf_op jit(solution)/shard_map/ppermute | solution.py:191
  62.6 20.7 %all-to-all-start.2 = ((bf16[32,112,128]{2,1,0:T(8,128)(2,1)}), bf16[32,112,128]{2,1,0:T(8,128)(2,1)S(1)}, u32[]{:S(2)}, u32[]{:S(2)}) async-start(bf16[32,112,128]{2,1,0:T(8,128)(2,1)} %cross.1), calls=%async_computation.2 | async-start | bytes 1835008 | tf_op jit(solution)/shard_map/all_to_all | solution.py:195

commit v5 on v4

--- a/solution.py
+++ b/solution.py
@@ -184,7 +184,7 @@
 
 
 def line(array, shift):
-    return lax.ppermute(array, "z", [(at, (at + shift) % 4) for at in range(4)])
+    return lax.ppermute(array, "z", [(at, at ^ shift) for at in range(4)])
 
 
 def swap(array):

time: 86.3 us -> 85.7 us (level)
  starting transfers between devices: 36 us -> 34.8 us
where the time goes in v5:
time: 85.7 us; the launch traced here: 85.3 us
  starting transfers between devices  34.8 us (41%)
  waiting for transfers between devices  34.6 us (40%)
  Pallas kernels  7.75 us (9%)
  between operations  4.88 us (6%)
  other arithmetic  1.85 us (2%)
  local copies, waits for them, and re-layouts  1.36 us (2%)
    all_to_all x3, starting transfers between devices, spread(): return lax.all_to_all(array, PLANE, 0, 0, tiled=True)  20.9 us
    all_to_all x3, waiting for transfers between devices, spread(): return lax.all_to_all(array, PLANE, 0, 0, tiled=True)  20.5 us
    ppermute x2, starting transfers between devices, swap(): return lax.ppermute(array, 'day', [(0, 1), (1, 0)])  9.15 us
    ppermute x3, waiting for transfers between devices, line(): return lax.ppermute(array, 'z', [(at, at ^ shift) for at in range(4)])  8.94 us
    ppermute x2, waiting for transfers between devices, swap(): return lax.ppermute(array, 'day', [(0, 1), (1, 0)])  5.16 us
    ppermute x3, starting transfers between devices, line(): return lax.ppermute(array, 'z', [(at, at ^ shift) for at in range(4)])  4.72 us
    pallas_call x1, Pallas kernels, prep(): pl.pallas_call(prep_kernel, out_shape=(jax.ShapeDtypeStruct((SIDE, ROWS,...  3.39 us
    pallas_call x1, Pallas kernels, lag(): pl.pallas_call(kernel, out_shape=jax.ShapeDtypeStruct((STEPS, 16, 32, LAG...  2.59 us
  transfers between devices with their start and end apart: 8, of which 6 were waited for; matrix products, arithmetic and copies ran while one was open for 4% of the time, Pallas kernels for 0%

profile of v5, /device:TPU:1, one launch (start us, length us, event | category | flops | bytes accessed | tf_op | source)
XLA Modules:
  0.0 85.3 jit_solution(5565254543635027328)
XLA Ops:
  0.0 3.4 %prep.1 = (bf16[32,112,128]{2,1,0:T(8,128)(2,1)}, bf16[1600,128]{1,0:T(8,128)(2,1)}) custom-call(bf16[32,32,400]{2,1,0:T(8,128)(2,1)} %spectra_ref.1), custom_call_target="tpu_custom_call" | custom-call | tf_op jit(solution)/shard_map/prep/pallas_call | solution.py:75
  3.4 0.0 copy-start.1
  3.4 8.7 %all-to-all-start = ((bf16[32,112,128]{2,1,0:T(8,128)(2,1)}), bf16[32,112,128]{2,1,0:T(8,128)(2,1)S(1)}, u32[]{:S(2)}, u32[]{:S(2)}) async-start(bf16[32,112,128]{2,1,0:T(8,128)(2,1)} %get-tuple-element.9), calls=%async_computation | async-start | bytes 1835008 | tf_op jit(solution)/shard_map/all_to_all | solution.py:195
  12.1 0.0 copy-start
  12.2 0.0 copy-done.1
  12.2 7.0 %collective-permute-start = (bf16[1600,128]{1,0:T(8,128)(2,1)S(1)}, bf16[1600,128]{1,0:T(8,128)(2,1)S(1)}, u32[]{:S(2)}, u32[]{:S(2)}) collective-permute-start(bf16[1600,128]{1,0:T(8,128)(2,1)S(1)} %copy-done.1), channel_id=1, source_target_pairs={{0,1},{1,0},{2,3},{3,2},{4,5},{5,4},{6,7},{7,6},{8,9},{9,8},{10,11... | collective-permute-start | bytes 1228808 | tf_op jit(solution)/shard_map/ppermute | solution.py:191
  19.2 0.0 copy-done
  19.2 0.6 fusion.5
  24.5 3.2 %all-to-all-done.own_ref = bf16[32,112,128]{2,1,0:T(8,128)(2,1)S(1)} async-done(((bf16[32,112,128]{2,1,0:T(8,128)(2,1)}), bf16[32,112,128]{2,1,0:T(8,128)(2,1)S(1)}, u32[]{:S(2)}, u32[]{:S(2)}) %all-to-all-start) | async-done | bytes 917536 | tf_op jit(solution)/shard_map/all_to_all | solution.py:195
  27.8 1.7 %collective-permute-start.1 = (bf16[2,112,128]{2,1,0:T(8,128)(2,1)S(1)}, bf16[2,112,128]{2,1,0:T(8,128)(2,1)S(1)}, u32[]{:S(2)}, u32[]{:S(2)}) collective-permute-start(bf16[2,112,128]{2,1,0:T(8,128)(2,1)S(1)} %pad_maximum_fusion.1), channel_id=1, source_target_pairs={{0,64},{64,0},{128,192},{192,128},{1,65},{65,1},{129,193},{193,129... | collective-permute-start | bytes 172040 | tf_op jit(solution)/shard_map/ppermute | solution.py:187
  29.5 3.0 %collective-permute-start.2 = (bf16[2,112,128]{2,1,0:T(8,128)(2,1)S(1)}, bf16[2,112,128]{2,1,0:T(8,128)(2,1)S(1)}, u32[]{:S(2)}, u32[]{:S(2)}) collective-permute-start(bf16[2,112,128]{2,1,0:T(8,128)(2,1)S(1)} %pad_maximum_fusion.1), channel_id=1, source_target_pairs={{0,128},{64,192},{128,0},{192,64},{1,129},{65,193},{129,1},{193,65... | collective-permute-start | bytes 172040 | tf_op jit(solution)/shard_map/ppermute | solution.py:187
  32.5 0.0 collective-permute-start.3
  32.5 0.0 collective-permute-done
  32.5 0.8 pad.4
  33.3 6.9 %collective-permute-done.1 = bf16[2,112,128]{2,1,0:T(8,128)(2,1)S(1)} collective-permute-done((bf16[2,112,128]{2,1,0:T(8,128)(2,1)S(1)}, bf16[2,112,128]{2,1,0:T(8,128)(2,1)S(1)}, u32[]{:S(2)}, u32[]{:S(2)}) %collective-permute-start.1) | collective-permute-done | bytes 57376 | tf_op jit(solution)/shard_map/ppermute | solution.py:187
  40.2 0.0 collective-permute-done.2
  40.2 2.0 %collective-permute-done.3 = bf16[2,112,128]{2,1,0:T(8,128)(2,1)S(1)} collective-permute-done((bf16[2,112,128]{2,1,0:T(8,128)(2,1)S(1)}, bf16[2,112,128]{2,1,0:T(8,128)(2,1)S(1)}, u32[]{:S(2)}, u32[]{:S(2)}) %collective-permute-start.3) | collective-permute-done | bytes 57376 | tf_op jit(solution)/shard_map/ppermute | solution.py:187
  42.2 7.6 %all-to-all-start.1 = ((bf16[32,56,128]{2,1,0:T(8,128)(2,1)}), bf16[32,56,128]{2,1,0:T(8,128)(2,1)S(1)}, u32[]{:S(2)}, u32[]{:S(2)}) async-start(bf16[32,56,128]{2,1,0:T(8,128)(2,1)} %bitcast), calls=%async_computation.1 | async-start | bytes 917504 | tf_op jit(solution)/shard_map/all_to_all | solution.py:195
  49.9 2.2 %collective-permute-start.4 = (bf16[2,112,128]{2,1,0:T(8,128)(2,1)S(1)}, bf16[2,112,128]{2,1,0:T(8,128)(2,1)S(1)}, u32[]{:S(2)}, u32[]{:S(2)}) collective-permute-start(bf16[2,112,128]{2,1,0:T(8,128)(2,1)S(1)} %add_add_fusion.mine_ref), channel_id=1, source_target_pairs={{0,1},{1,0},{2,3},{3,2},{4,5},{5,4},{6,7},{7,6},{8,9},{9,8},{10,11... | collective-permute-start | bytes 172040 | tf_op jit(solution)/shard_map/ppermute | solution.py:191
  52.0 5.2 %collective-permute-done.4.away_ref = bf16[2,112,128]{2,1,0:T(8,128)(2,1)S(1)} collective-permute-done((bf16[2,112,128]{2,1,0:T(8,128)(2,1)S(1)}, bf16[2,112,128]{2,1,0:T(8,128)(2,1)S(1)}, u32[]{:S(2)}, u32[]{:S(2)}) %collective-permute-start.4) | collective-permute-done | bytes 57376 | tf_op jit(solution)/shard_map/ppermute | solution.py:191
  57.2 3.6 %all-to-all-done.1.other_ref = bf16[32,56,128]{2,1,0:T(8,128)(2,1)S(1)} async-done(((bf16[32,56,128]{2,1,0:T(8,128)(2,1)}), bf16[32,56,128]{2,1,0:T(8,128)(2,1)S(1)}, u32[]{:S(2)}, u32[]{:S(2)}) %all-to-all-start.1) | async-done | bytes 458784 | tf_op jit(solution)/shard_map/all_to_all | solution.py:195
  60.8 1.8 %cross.1 = bf16[32,112,128]{2,1,0:T(8,128)(2,1)} custom-call(bf16[32,112,128]{2,1,0:T(8,128)(2,1)S(1)} %all-to-all-done.own_ref, bf16[32,56,128]{2,1,0:T(8,128)(2,1)S(1)} %all-to-all-done.1.other_ref, bf16[2,112,128]{2,1,0:T(8,128)(2,1)S(1)} %add_add_fusion.mine_ref, bf16[2,112,128]{2,1,0:T(8,128)(2,1)S(1)} %collective-permute-done.4.away_ref), custom_call_target="tpu_custom_call" | custom-call | tf_op jit(solution)/shard_map/cross/pallas_call | solution.py:150
  62.6 4.6 %all-to-all-start.2 = ((bf16[32,112,128]{2,1,0:T(8,128)(2,1)}), bf16[32,112,128]{2,1,0:T(8,128)(2,1)S(1)}, u32[]{:S(2)}, u32[]{:S(2)}) async-start(bf16[32,112,128]{2,1,0:T(8,128)(2,1)} %cross.1), calls=%async_computation.2 | async-start | bytes 1835008 | tf_op jit(solution)/shard_map/all_to_all | solution.py:195
  67.2 1.8 %cosine_convert_fusion = (bf16[1,200,400]{2,1,0:T(8,128)(2,1)S(1)}, bf16[1,200,400]{2,1,0:T(8,128)(2,1)S(1)}) fusion(s32[400]{0:T(512)S(1)} %iota_add_fusion), kind=kLoop, calls=%fused_computation.5 | loop fusion | flops 960000 | bytes 321600 | tf_op jit(solution)/shard_map/convert
  69.0 0.1 pad_maximum_fusion.refs_1_
  69.0 13.6 %all-to-all-done.2.refs_0_ = bf16[32,112,128]{2,1,0:T(8,128)(2,1)S(1)} async-done(((bf16[32,112,128]{2,1,0:T(8,128)(2,1)}), bf16[32,112,128]{2,1,0:T(8,128)(2,1)S(1)}, u32[]{:S(2)}, u32[]{:S(2)}) %all-to-all-start.2) | async-done | bytes 917536 | tf_op jit(solution)/shard_map/all_to_all | solution.py:195
  82.7 2.6 %lag.1 = bf16[2,16,32,400]{3,2,1,0:T(8,128)(2,1)} custom-call(bf16[32,112,128]{2,1,0:T(8,128)(2,1)S(1)} %all-to-all-done.2.refs_0_, bf16[2,200,400]{2,1,0:T(8,128)(2,1)S(1)} %pad_maximum_fusion.refs_1_), custom_call_target="tpu_custom_call" | custom-call | tf_op jit(solution)/shard_map/lag/pallas_call | solution.py:175
  (4 shorter events, 0.0 us)
Async XLA Ops:
  3.4 8.8 %copy-start.1 = (bf16[1600,128]{1,0:T(8,128)(2,1)S(1)}, bf16[1600,128]{1,0:T(8,128)(2,1)}, u32[]{:S(2)}) copy-start(bf16[1600,128]{1,0:T(8,128)(2,1)} %get-tuple-element.10) | copy-start | bytes 1228804
  3.4 24.3 %all-to-all-start = ((bf16[32,112,128]{2,1,0:T(8,128)(2,1)}), bf16[32,112,128]{2,1,0:T(8,128)(2,1)S(1)}, u32[]{:S(2)}, u32[]{:S(2)}) async-start(bf16[32,112,128]{2,1,0:T(8,128)(2,1)} %get-tuple-element.9), calls=%async_computation | async-start | bytes 1835008 | tf_op jit(solution)/shard_map/all_to_all | solution.py:195
  12.1 7.0 %copy-start = (s32[2]{0:T(128)S(1)}, s32[2]{0:T(128)}, u32[]{:S(2)}) copy-start(s32[2]{0:T(128)} %param.3) | copy-start | bytes 28
  12.2 20.3 %collective-permute-start = (bf16[1600,128]{1,0:T(8,128)(2,1)S(1)}, bf16[1600,128]{1,0:T(8,128)(2,1)S(1)}, u32[]{:S(2)}, u32[]{:S(2)}) collective-permute-start(bf16[1600,128]{1,0:T(8,128)(2,1)S(1)} %copy-done.1), channel_id=1, source_target_pairs={{0,1},{1,0},{2,3},{3,2},{4,5},{5,4},{6,7},{7,6},{8,9},{9,8},{10,11... | collective-permute-start | bytes 1228808 | tf_op jit(solution)/shard_map/ppermute | solution.py:191
  27.8 12.5 %collective-permute-start.1 = (bf16[2,112,128]{2,1,0:T(8,128)(2,1)S(1)}, bf16[2,112,128]{2,1,0:T(8,128)(2,1)S(1)}, u32[]{:S(2)}, u32[]{:S(2)}) collective-permute-start(bf16[2,112,128]{2,1,0:T(8,128)(2,1)S(1)} %pad_maximum_fusion.1), channel_id=1, source_target_pairs={{0,64},{64,0},{128,192},{192,128},{1,65},{65,1},{129,193},{193,129... | collective-permute-start | bytes 172040 | tf_op jit(solution)/shard_map/ppermute | solution.py:187
  29.5 10.7 %collective-permute-start.2 = (bf16[2,112,128]{2,1,0:T(8,128)(2,1)S(1)}, bf16[2,112,128]{2,1,0:T(8,128)(2,1)S(1)}, u32[]{:S(2)}, u32[]{:S(2)}) collective-permute-start(bf16[2,112,128]{2,1,0:T(8,128)(2,1)S(1)} %pad_maximum_fusion.1), channel_id=1, source_target_pairs={{0,128},{64,192},{128,0},{192,64},{1,129},{65,193},{129,1},{193,65... | collective-permute-start | bytes 172040 | tf_op jit(solution)/shard_map/ppermute | solution.py:187
  32.5 9.8 %collective-permute-start.3 = (bf16[2,112,128]{2,1,0:T(8,128)(2,1)S(1)}, bf16[2,112,128]{2,1,0:T(8,128)(2,1)S(1)}, u32[]{:S(2)}, u32[]{:S(2)}) collective-permute-start(bf16[2,112,128]{2,1,0:T(8,128)(2,1)S(1)} %pad_maximum_fusion.1), channel_id=1, source_target_pairs={{0,192},{64,128},{128,64},{192,0},{1,193},{65,129},{129,65},{193,1... | collective-permute-start | bytes 172040 | tf_op jit(solution)/shard_map/ppermute | solution.py:187
  42.2 18.6 %all-to-all-start.1 = ((bf16[32,56,128]{2,1,0:T(8,128)(2,1)}), bf16[32,56,128]{2,1,0:T(8,128)(2,1)S(1)}, u32[]{:S(2)}, u32[]{:S(2)}) async-start(bf16[32,56,128]{2,1,0:T(8,128)(2,1)} %bitcast), calls=%async_computation.1 | async-start | bytes 917504 | tf_op jit(solution)/shard_map/all_to_all | solution.py:195
  49.9 7.3 %collective-permute-start.4 = (bf16[2,112,128]{2,1,0:T(8,128)(2,1)S(1)}, bf16[2,112,128]{2,1,0:T(8,128)(2,1)S(1)}, u32[]{:S(2)}, u32[]{:S(2)}) collective-permute-start(bf16[2,112,128]{2,1,0:T(8,128)(2,1)S(1)} %add_add_fusion.mine_ref), channel_id=1, source_target_pairs={{0,1},{1,0},{2,3},{3,2},{4,5},{5,4},{6,7},{7,6},{8,9},{9,8},{10,11... | collective-permute-start | bytes 172040 | tf_op jit(solution)/shard_map/ppermute | solution.py:191
  62.6 20.1 %all-to-all-start.2 = ((bf16[32,112,128]{2,1,0:T(8,128)(2,1)}), bf16[32,112,128]{2,1,0:T(8,128)(2,1)S(1)}, u32[]{:S(2)}, u32[]{:S(2)}) async-start(bf16[32,112,128]{2,1,0:T(8,128)(2,1)} %cross.1), calls=%async_computation.2 | async-start | bytes 1835008 | tf_op jit(solution)/shard_map/all_to_all | solution.py:195

commit v6 on v5

--- a/solution.py
+++ b/solution.py
@@ -183,6 +183,21 @@
     )(summed, table)
 
 
+def pad_kernel(in_ref, out_ref):
+    out_ref[: BINS * 8, :] = in_ref[...]
+    out_ref[BINS * 8 :, :] = jnp.zeros((SIDE * HALF - BINS * 8, 128), jnp.bfloat16)
+
+
+def pad(array):
+    return pl.pallas_call(
+        pad_kernel,
+        out_shape=jax.ShapeDtypeStruct((SIDE * HALF, 128), jnp.bfloat16),
+        in_specs=[VMEM],
+        out_specs=VMEM,
+        name="pad",
+    )(array).reshape(SIDE, HALF, 128)
+
+
 def line(array, shift):
     return lax.ppermute(array, "z", [(at, at ^ shift) for at in range(4)])
 
@@ -206,7 +221,7 @@
         pieces.append(jnp.where(owners[step] // SIDE == z_lo, piece, jnp.zeros_like(piece)))
     held = jnp.stack(pieces)
     block = held + line(held, 1) + line(held, 2) + line(held, 3)
-    arrived = jnp.pad(arrived, ((0, SIDE * HALF - BINS * 8), (0, 0))).reshape(SIDE, HALF, 128)
+    arrived = pad(arrived)
     arrived, block = lax.optimization_barrier((arrived, block))
     other = spread(arrived)
     home = spread(cross(own, other, block, swap(block)))

time: 85.7 us -> 85.8 us (level)
  waiting for transfers between devices: 34.6 us -> 31.5 us
  Pallas kernels: 7.75 us -> 9.54 us
  starting transfers between devices: 34.8 us -> 35.9 us
    pallas_call x0 -> x1, Pallas kernels: none -> 1.8 us  [pad(): pl.pallas_call(pad_kernel, out_shape=jax.ShapeDtypeStruct((SIDE * HALF, 1...]
    ppermute x3, waiting for transfers between devices: 8.94 us -> 7.19 us  [line(): return lax.ppermute(array, 'z', [(at, at ^ shift) for at in range(4)])]
    ppermute x2, starting transfers between devices: 9.15 us -> 10.2 us  [swap(): return lax.ppermute(array, 'day', [(0, 1), (1, 0)])]
    ppermute x2, waiting for transfers between devices: 5.16 us -> 4.09 us  [swap(): return lax.ppermute(array, 'day', [(0, 1), (1, 0)])]
  transfers between devices with their start and end apart: 8 -> 8, of which waited for: 6 -> 6; matrix products, arithmetic and copies ran while one was open for 4% -> 3% of each run, Pallas kernels for 0% -> 2%
where the time goes in v6:
time: 85.8 us; the launch traced here: 85.3 us
  starting transfers between devices  35.9 us (42%)
  waiting for transfers between devices  31.5 us (37%)
  Pallas kernels  9.54 us (11%)
  between operations  5.08 us (6%)
  other arithmetic  1.85 us (2%)
  local copies, waits for them, and re-layouts  1.42 us (2%)
    all_to_all x3, starting transfers between devices, spread(): return lax.all_to_all(array, PLANE, 0, 0, tiled=True)  20.9 us
    all_to_all x3, waiting for transfers between devices, spread(): return lax.all_to_all(array, PLANE, 0, 0, tiled=True)  20.2 us
    ppermute x2, starting transfers between devices, swap(): return lax.ppermute(array, 'day', [(0, 1), (1, 0)])  10.2 us
    ppermute x3, waiting for transfers between devices, line(): return lax.ppermute(array, 'z', [(at, at ^ shift) for at in range(4)])  7.19 us
    ppermute x3, starting transfers between devices, line(): return lax.ppermute(array, 'z', [(at, at ^ shift) for at in range(4)])  4.72 us
    ppermute x2, waiting for transfers between devices, swap(): return lax.ppermute(array, 'day', [(0, 1), (1, 0)])  4.09 us
    pallas_call x1, Pallas kernels, prep(): pl.pallas_call(prep_kernel, out_shape=(jax.ShapeDtypeStruct((SIDE, ROWS,...  3.39 us
    pallas_call x1, Pallas kernels, lag(): pl.pallas_call(kernel, out_shape=jax.ShapeDtypeStruct((STEPS, 16, 32, LAG...  2.6 us
  transfers between devices with their start and end apart: 8, of which 6 were waited for; matrix products, arithmetic and copies ran while one was open for 3% of the time, Pallas kernels for 2%

profile of v6, /device:TPU:1, one launch (start us, length us, event | category | flops | bytes accessed | tf_op | source)
XLA Modules:
  0.0 85.3 jit_solution(14755138955530042006)
XLA Ops:
  0.0 3.4 %prep.1 = (bf16[32,112,128]{2,1,0:T(8,128)(2,1)}, bf16[1600,128]{1,0:T(8,128)(2,1)}) custom-call(bf16[32,32,400]{2,1,0:T(8,128)(2,1)} %spectra_ref.1), custom_call_target="tpu_custom_call" | custom-call | tf_op jit(solution)/shard_map/prep/pallas_call | solution.py:75
  3.4 0.0 copy-start.2
  3.4 8.7 %all-to-all-start = ((bf16[32,112,128]{2,1,0:T(8,128)(2,1)}), bf16[32,112,128]{2,1,0:T(8,128)(2,1)S(1)}, u32[]{:S(2)}, u32[]{:S(2)}) async-start(bf16[32,112,128]{2,1,0:T(8,128)(2,1)} %get-tuple-element.9), calls=%async_computation | async-start | bytes 1835008 | tf_op jit(solution)/shard_map/all_to_all | solution.py:210
  12.1 0.0 copy-start.1
  12.2 0.0 copy-done.2
  12.2 7.0 %collective-permute-start = (bf16[1600,128]{1,0:T(8,128)(2,1)S(1)}, bf16[1600,128]{1,0:T(8,128)(2,1)S(1)}, u32[]{:S(2)}, u32[]{:S(2)}) collective-permute-start(bf16[1600,128]{1,0:T(8,128)(2,1)S(1)} %copy-done.2), channel_id=1, source_target_pairs={{0,1},{1,0},{2,3},{3,2},{4,5},{5,4},{6,7},{7,6},{8,9},{9,8},{10,11... | collective-permute-start | bytes 1228808 | tf_op jit(solution)/shard_map/ppermute | solution.py:206
  19.2 0.0 copy-done.1
  19.2 0.7 fusion.5
  24.8 2.9 %all-to-all-done.own_ref = bf16[32,112,128]{2,1,0:T(8,128)(2,1)S(1)} async-done(((bf16[32,112,128]{2,1,0:T(8,128)(2,1)}), bf16[32,112,128]{2,1,0:T(8,128)(2,1)S(1)}, u32[]{:S(2)}, u32[]{:S(2)}) %all-to-all-start) | async-done | bytes 917536 | tf_op jit(solution)/shard_map/all_to_all | solution.py:210
  27.8 1.7 %collective-permute-start.1 = (bf16[2,112,128]{2,1,0:T(8,128)(2,1)S(1)}, bf16[2,112,128]{2,1,0:T(8,128)(2,1)S(1)}, u32[]{:S(2)}, u32[]{:S(2)}) collective-permute-start(bf16[2,112,128]{2,1,0:T(8,128)(2,1)S(1)} %pad_maximum_fusion.1), channel_id=1, source_target_pairs={{0,64},{64,0},{128,192},{192,128},{1,65},{65,1},{129,193},{193,129... | collective-permute-start | bytes 172040 | tf_op jit(solution)/shard_map/ppermute | solution.py:202
  29.5 3.0 %collective-permute-start.2 = (bf16[2,112,128]{2,1,0:T(8,128)(2,1)S(1)}, bf16[2,112,128]{2,1,0:T(8,128)(2,1)S(1)}, u32[]{:S(2)}, u32[]{:S(2)}) collective-permute-start(bf16[2,112,128]{2,1,0:T(8,128)(2,1)S(1)} %pad_maximum_fusion.1), channel_id=1, source_target_pairs={{0,128},{64,192},{128,0},{192,64},{1,129},{65,193},{129,1},{193,65... | collective-permute-start | bytes 172040 | tf_op jit(solution)/shard_map/ppermute | solution.py:202
  32.5 0.0 collective-permute-start.3
  32.5 0.0 collective-permute-done.in_ref
  32.5 0.0 copy-start
  32.5 0.8 copy-done
  33.2 1.8 %pad.13 = bf16[1792,128]{1,0:T(8,128)(2,1)} custom-call(bf16[1600,128]{1,0:T(8,128)(2,1)} %copy-done), custom_call_target="tpu_custom_call" | custom-call | tf_op jit(solution)/shard_map/pad/pallas_call | solution.py:192
  35.0 5.2 %collective-permute-done.1 = bf16[2,112,128]{2,1,0:T(8,128)(2,1)S(1)} collective-permute-done((bf16[2,112,128]{2,1,0:T(8,128)(2,1)S(1)}, bf16[2,112,128]{2,1,0:T(8,128)(2,1)S(1)}, u32[]{:S(2)}, u32[]{:S(2)}) %collective-permute-start.1) | collective-permute-done | bytes 57376 | tf_op jit(solution)/shard_map/ppermute | solution.py:202
  40.2 0.0 collective-permute-done.2
  40.2 2.0 %collective-permute-done.3 = bf16[2,112,128]{2,1,0:T(8,128)(2,1)S(1)} collective-permute-done((bf16[2,112,128]{2,1,0:T(8,128)(2,1)S(1)}, bf16[2,112,128]{2,1,0:T(8,128)(2,1)S(1)}, u32[]{:S(2)}, u32[]{:S(2)}) %collective-permute-start.3) | collective-permute-done | bytes 57376 | tf_op jit(solution)/shard_map/ppermute | solution.py:202
  42.2 7.6 %all-to-all-start.1 = ((bf16[32,56,128]{2,1,0:T(8,128)(2,1)}), bf16[32,56,128]{2,1,0:T(8,128)(2,1)S(1)}, u32[]{:S(2)}, u32[]{:S(2)}) async-start(bf16[32,56,128]{2,1,0:T(8,128)(2,1)} %bitcast.3), calls=%async_computation.1 | async-start | bytes 917504 | tf_op jit(solution)/shard_map/all_to_all | solution.py:210
  49.9 3.2 %collective-permute-start.4 = (bf16[2,112,128]{2,1,0:T(8,128)(2,1)S(1)}, bf16[2,112,128]{2,1,0:T(8,128)(2,1)S(1)}, u32[]{:S(2)}, u32[]{:S(2)}) collective-permute-start(bf16[2,112,128]{2,1,0:T(8,128)(2,1)S(1)} %add_add_fusion.mine_ref), channel_id=1, source_target_pairs={{0,1},{1,0},{2,3},{3,2},{4,5},{5,4},{6,7},{7,6},{8,9},{9,8},{10,11... | collective-permute-start | bytes 172040 | tf_op jit(solution)/shard_map/ppermute | solution.py:206
  53.1 4.1 %collective-permute-done.4.away_ref = bf16[2,112,128]{2,1,0:T(8,128)(2,1)S(1)} collective-permute-done((bf16[2,112,128]{2,1,0:T(8,128)(2,1)S(1)}, bf16[2,112,128]{2,1,0:T(8,128)(2,1)S(1)}, u32[]{:S(2)}, u32[]{:S(2)}) %collective-permute-start.4) | collective-permute-done | bytes 57376 | tf_op jit(solution)/shard_map/ppermute | solution.py:206
  57.2 3.6 %all-to-all-done.1.other_ref = bf16[32,56,128]{2,1,0:T(8,128)(2,1)S(1)} async-done(((bf16[32,56,128]{2,1,0:T(8,128)(2,1)}), bf16[32,56,128]{2,1,0:T(8,128)(2,1)S(1)}, u32[]{:S(2)}, u32[]{:S(2)}) %all-to-all-start.1) | async-done | bytes 458784 | tf_op jit(solution)/shard_map/all_to_all | solution.py:210
  60.8 1.8 %cross.1 = bf16[32,112,128]{2,1,0:T(8,128)(2,1)} custom-call(bf16[32,112,128]{2,1,0:T(8,128)(2,1)S(1)} %all-to-all-done.own_ref, bf16[32,56,128]{2,1,0:T(8,128)(2,1)S(1)} %all-to-all-done.1.other_ref, bf16[2,112,128]{2,1,0:T(8,128)(2,1)S(1)} %add_add_fusion.mine_ref, bf16[2,112,128]{2,1,0:T(8,128)(2,1)S(1)} %collective-permute-done.4.away_ref), custom_call_target="tpu_custom_call" | custom-call | tf_op jit(solution)/shard_map/cross/pallas_call | solution.py:150
  62.6 4.6 %all-to-all-start.2 = ((bf16[32,112,128]{2,1,0:T(8,128)(2,1)}), bf16[32,112,128]{2,1,0:T(8,128)(2,1)S(1)}, u32[]{:S(2)}, u32[]{:S(2)}) async-start(bf16[32,112,128]{2,1,0:T(8,128)(2,1)} %cross.1), calls=%async_computation.2 | async-start | bytes 1835008 | tf_op jit(solution)/shard_map/all_to_all | solution.py:210
  67.2 1.8 %cosine_convert_fusion = (bf16[1,200,400]{2,1,0:T(8,128)(2,1)S(1)}, bf16[1,200,400]{2,1,0:T(8,128)(2,1)S(1)}) fusion(s32[400]{0:T(512)S(1)} %iota_add_fusion), kind=kLoop, calls=%fused_computation.5 | loop fusion | flops 960000 | bytes 321600 | tf_op jit(solution)/shard_map/convert
  69.0 0.1 pad_maximum_fusion.refs_1_
  69.0 13.6 %all-to-all-done.2.refs_0_ = bf16[32,112,128]{2,1,0:T(8,128)(2,1)S(1)} async-done(((bf16[32,112,128]{2,1,0:T(8,128)(2,1)}), bf16[32,112,128]{2,1,0:T(8,128)(2,1)S(1)}, u32[]{:S(2)}, u32[]{:S(2)}) %all-to-all-start.2) | async-done | bytes 917536 | tf_op jit(solution)/shard_map/all_to_all | solution.py:210
  82.7 2.6 %lag.1 = bf16[2,16,32,400]{3,2,1,0:T(8,128)(2,1)} custom-call(bf16[32,112,128]{2,1,0:T(8,128)(2,1)S(1)} %all-to-all-done.2.refs_0_, bf16[2,200,400]{2,1,0:T(8,128)(2,1)S(1)} %pad_maximum_fusion.refs_1_), custom_call_target="tpu_custom_call" | custom-call | tf_op jit(solution)/shard_map/lag/pallas_call | solution.py:175
  (4 shorter events, 0.0 us)
Async XLA Ops:
  3.4 8.8 %copy-start.2 = (bf16[1600,128]{1,0:T(8,128)(2,1)S(1)}, bf16[1600,128]{1,0:T(8,128)(2,1)}, u32[]{:S(2)}) copy-start(bf16[1600,128]{1,0:T(8,128)(2,1)} %get-tuple-element.10) | copy-start | bytes 1228804
  3.4 24.3 %all-to-all-start = ((bf16[32,112,128]{2,1,0:T(8,128)(2,1)}), bf16[32,112,128]{2,1,0:T(8,128)(2,1)S(1)}, u32[]{:S(2)}, u32[]{:S(2)}) async-start(bf16[32,112,128]{2,1,0:T(8,128)(2,1)} %get-tuple-element.9), calls=%async_computation | async-start | bytes 1835008 | tf_op jit(solution)/shard_map/all_to_all | solution.py:210
  12.1 7.0 %copy-start.1 = (s32[2]{0:T(128)S(1)}, s32[2]{0:T(128)}, u32[]{:S(2)}) copy-start(s32[2]{0:T(128)} %param.3) | copy-start | bytes 28
  12.2 20.3 %collective-permute-start = (bf16[1600,128]{1,0:T(8,128)(2,1)S(1)}, bf16[1600,128]{1,0:T(8,128)(2,1)S(1)}, u32[]{:S(2)}, u32[]{:S(2)}) collective-permute-start(bf16[1600,128]{1,0:T(8,128)(2,1)S(1)} %copy-done.2), channel_id=1, source_target_pairs={{0,1},{1,0},{2,3},{3,2},{4,5},{5,4},{6,7},{7,6},{8,9},{9,8},{10,11... | collective-permute-start | bytes 1228808 | tf_op jit(solution)/shard_map/ppermute | solution.py:206
  27.8 12.5 %collective-permute-start.1 = (bf16[2,112,128]{2,1,0:T(8,128)(2,1)S(1)}, bf16[2,112,128]{2,1,0:T(8,128)(2,1)S(1)}, u32[]{:S(2)}, u32[]{:S(2)}) collective-permute-start(bf16[2,112,128]{2,1,0:T(8,128)(2,1)S(1)} %pad_maximum_fusion.1), channel_id=1, source_target_pairs={{0,64},{64,0},{128,192},{192,128},{1,65},{65,1},{129,193},{193,129... | collective-permute-start | bytes 172040 | tf_op jit(solution)/shard_map/ppermute | solution.py:202
  29.5 10.7 %collective-permute-start.2 = (bf16[2,112,128]{2,1,0:T(8,128)(2,1)S(1)}, bf16[2,112,128]{2,1,0:T(8,128)(2,1)S(1)}, u32[]{:S(2)}, u32[]{:S(2)}) collective-permute-start(bf16[2,112,128]{2,1,0:T(8,128)(2,1)S(1)} %pad_maximum_fusion.1), channel_id=1, source_target_pairs={{0,128},{64,192},{128,0},{192,64},{1,129},{65,193},{129,1},{193,65... | collective-permute-start | bytes 172040 | tf_op jit(solution)/shard_map/ppermute | solution.py:202
  32.5 9.8 %collective-permute-start.3 = (bf16[2,112,128]{2,1,0:T(8,128)(2,1)S(1)}, bf16[2,112,128]{2,1,0:T(8,128)(2,1)S(1)}, u32[]{:S(2)}, u32[]{:S(2)}) collective-permute-start(bf16[2,112,128]{2,1,0:T(8,128)(2,1)S(1)} %pad_maximum_fusion.1), channel_id=1, source_target_pairs={{0,192},{64,128},{128,64},{192,0},{1,193},{65,129},{129,65},{193,1... | collective-permute-start | bytes 172040 | tf_op jit(solution)/shard_map/ppermute | solution.py:202
  32.5 0.8 copy-start
  42.2 18.6 %all-to-all-start.1 = ((bf16[32,56,128]{2,1,0:T(8,128)(2,1)}), bf16[32,56,128]{2,1,0:T(8,128)(2,1)S(1)}, u32[]{:S(2)}, u32[]{:S(2)}) async-start(bf16[32,56,128]{2,1,0:T(8,128)(2,1)} %bitcast.3), calls=%async_computation.1 | async-start | bytes 917504 | tf_op jit(solution)/shard_map/all_to_all | solution.py:210
  49.9 7.3 %collective-permute-start.4 = (bf16[2,112,128]{2,1,0:T(8,128)(2,1)S(1)}, bf16[2,112,128]{2,1,0:T(8,128)(2,1)S(1)}, u32[]{:S(2)}, u32[]{:S(2)}) collective-permute-start(bf16[2,112,128]{2,1,0:T(8,128)(2,1)S(1)} %add_add_fusion.mine_ref), channel_id=1, source_target_pairs={{0,1},{1,0},{2,3},{3,2},{4,5},{5,4},{6,7},{7,6},{8,9},{9,8},{10,11... | collective-permute-start | bytes 172040 | tf_op jit(solution)/shard_map/ppermute | solution.py:206
  62.6 20.1 %all-to-all-start.2 = ((bf16[32,112,128]{2,1,0:T(8,128)(2,1)}), bf16[32,112,128]{2,1,0:T(8,128)(2,1)S(1)}, u32[]{:S(2)}, u32[]{:S(2)}) async-start(bf16[32,112,128]{2,1,0:T(8,128)(2,1)} %cross.1), calls=%async_computation.2 | async-start | bytes 1835008 | tf_op jit(solution)/shard_map/all_to_all | solution.py:210

commit v7 on v5

--- a/solution.py
+++ b/solution.py
@@ -157,7 +157,8 @@
     )(own, other, mine, away)
 
 
-def lag_kernel(norm, summed_ref, table_ref, out_ref, rows_ref):
+def lag_kernel(norm, summed_ref, table_ref, out_ref, rows_ref, held_ref, sems):
+    started = []
     rows_ref[...] = summed_ref[...].astype(jnp.float32).reshape(SIDE * ROWS, 128)
     for i in range(16):
         turned = rows_ref[pl.ds(i, BINS, stride=16), :].T.astype(jnp.bfloat16)
@@ -165,7 +166,17 @@
         lagged = lagged + jnp.dot(turned[64:], table_ref[1], preferred_element_type=jnp.float32)
         lagged = (lagged * norm).astype(jnp.bfloat16)
         for step in range(STEPS):
-            out_ref[step, i] = lagged[step * 32 : step * 32 + 32]
+            held_ref[step, i] = lagged[step * 32 : step * 32 + 32]
+        if i % 4 == 3:
+            for step in range(STEPS):
+                part = pl.ds(i - 3, 4)
+                copy = pltpu.make_async_copy(
+                    held_ref.at[step, part], out_ref.at[step, part], sems.at[i // 4 * 2 + step]
+                )
+                copy.start()
+                started.append(copy)
+    for copy in started:
+        copy.wait()
 
 
 def lag(norm, summed, table):
@@ -176,8 +187,12 @@
         kernel,
         out_shape=jax.ShapeDtypeStruct((STEPS, 16, 32, LAGS), jnp.bfloat16),
         in_specs=[VMEM, VMEM],
-        out_specs=VMEM,
-        scratch_shapes=[pltpu.VMEM((SIDE * ROWS, 128), jnp.float32)],
+        out_specs=pl.BlockSpec(memory_space=pl.ANY),
+        scratch_shapes=[
+            pltpu.VMEM((SIDE * ROWS, 128), jnp.float32),
+            pltpu.VMEM((STEPS, 16, 32, LAGS), jnp.bfloat16),
+            pltpu.SemaphoreType.DMA((8,)),
+        ],
         compiler_params=ROOM,
         name="lag",
     )(summed, table)

time: 85.7 us -> 85.5 us (level)
  no operation moved by 1% of the time
where the time goes in v7:
time: 85.5 us; the launch traced here: 85.1 us
  starting transfers between devices  34.8 us (41%)
  waiting for transfers between devices  34.6 us (40%)
  Pallas kernels  7.55 us (9%)
  between operations  4.88 us (6%)
  other arithmetic  1.85 us (2%)
  local copies, waits for them, and re-layouts  1.36 us (2%)
    all_to_all x3, starting transfers between devices, spread(): return lax.all_to_all(array, PLANE, 0, 0, tiled=True)  20.9 us
    all_to_all x3, waiting for transfers between devices, spread(): return lax.all_to_all(array, PLANE, 0, 0, tiled=True)  20.5 us
    ppermute x2, starting transfers between devices, swap(): return lax.ppermute(array, 'day', [(0, 1), (1, 0)])  9.15 us
    ppermute x3, waiting for transfers between devices, line(): return lax.ppermute(array, 'z', [(at, at ^ shift) for at in range(4)])  8.94 us
    ppermute x2, waiting for transfers between devices, swap(): return lax.ppermute(array, 'day', [(0, 1), (1, 0)])  5.16 us
    ppermute x3, starting transfers between devices, line(): return lax.ppermute(array, 'z', [(at, at ^ shift) for at in range(4)])  4.72 us
    pallas_call x1, Pallas kernels, prep(): pl.pallas_call(prep_kernel, out_shape=(jax.ShapeDtypeStruct((SIDE, ROWS,...  3.39 us
    pallas_call x1, Pallas kernels, lag(): pl.pallas_call(kernel, out_shape=jax.ShapeDtypeStruct((STEPS, 16, 32, LAG...  2.4 us
  transfers between devices with their start and end apart: 8, of which 6 were waited for; matrix products, arithmetic and copies ran while one was open for 4% of the time, Pallas kernels for 0%

profile of v7, /device:TPU:1, one launch (start us, length us, event | category | flops | bytes accessed | tf_op | source)
XLA Modules:
  0.0 85.1 jit_solution(10477036118820990912)
XLA Ops:
  0.0 3.4 %prep.1 = (bf16[32,112,128]{2,1,0:T(8,128)(2,1)}, bf16[1600,128]{1,0:T(8,128)(2,1)}) custom-call(bf16[32,32,400]{2,1,0:T(8,128)(2,1)} %spectra_ref.1), custom_call_target="tpu_custom_call" | custom-call | tf_op jit(solution)/shard_map/prep/pallas_call | solution.py:75
  3.4 0.0 copy-start.1
  3.4 8.7 %all-to-all-start = ((bf16[32,112,128]{2,1,0:T(8,128)(2,1)}), bf16[32,112,128]{2,1,0:T(8,128)(2,1)S(1)}, u32[]{:S(2)}, u32[]{:S(2)}) async-start(bf16[32,112,128]{2,1,0:T(8,128)(2,1)} %get-tuple-element.9), calls=%async_computation | async-start | bytes 1835008 | tf_op jit(solution)/shard_map/all_to_all | solution.py:210
  12.1 0.0 copy-start
  12.2 0.0 copy-done.1
  12.2 7.0 %collective-permute-start = (bf16[1600,128]{1,0:T(8,128)(2,1)S(1)}, bf16[1600,128]{1,0:T(8,128)(2,1)S(1)}, u32[]{:S(2)}, u32[]{:S(2)}) collective-permute-start(bf16[1600,128]{1,0:T(8,128)(2,1)S(1)} %copy-done.1), channel_id=1, source_target_pairs={{0,1},{1,0},{2,3},{3,2},{4,5},{5,4},{6,7},{7,6},{8,9},{9,8},{10,11... | collective-permute-start | bytes 1228808 | tf_op jit(solution)/shard_map/ppermute | solution.py:206
  19.2 0.0 copy-done
  19.2 0.6 fusion.5
  24.5 3.2 %all-to-all-done.own_ref = bf16[32,112,128]{2,1,0:T(8,128)(2,1)S(1)} async-done(((bf16[32,112,128]{2,1,0:T(8,128)(2,1)}), bf16[32,112,128]{2,1,0:T(8,128)(2,1)S(1)}, u32[]{:S(2)}, u32[]{:S(2)}) %all-to-all-start) | async-done | bytes 917536 | tf_op jit(solution)/shard_map/all_to_all | solution.py:210
  27.8 1.7 %collective-permute-start.1 = (bf16[2,112,128]{2,1,0:T(8,128)(2,1)S(1)}, bf16[2,112,128]{2,1,0:T(8,128)(2,1)S(1)}, u32[]{:S(2)}, u32[]{:S(2)}) collective-permute-start(bf16[2,112,128]{2,1,0:T(8,128)(2,1)S(1)} %pad_maximum_fusion.1), channel_id=1, source_target_pairs={{0,64},{64,0},{128,192},{192,128},{1,65},{65,1},{129,193},{193,129... | collective-permute-start | bytes 172040 | tf_op jit(solution)/shard_map/ppermute | solution.py:202
  29.5 3.0 %collective-permute-start.2 = (bf16[2,112,128]{2,1,0:T(8,128)(2,1)S(1)}, bf16[2,112,128]{2,1,0:T(8,128)(2,1)S(1)}, u32[]{:S(2)}, u32[]{:S(2)}) collective-permute-start(bf16[2,112,128]{2,1,0:T(8,128)(2,1)S(1)} %pad_maximum_fusion.1), channel_id=1, source_target_pairs={{0,128},{64,192},{128,0},{192,64},{1,129},{65,193},{129,1},{193,65... | collective-permute-start | bytes 172040 | tf_op jit(solution)/shard_map/ppermute | solution.py:202
  32.5 0.0 collective-permute-start.3
  32.5 0.0 collective-permute-done
  32.5 0.8 pad.4
  33.3 6.9 %collective-permute-done.1 = bf16[2,112,128]{2,1,0:T(8,128)(2,1)S(1)} collective-permute-done((bf16[2,112,128]{2,1,0:T(8,128)(2,1)S(1)}, bf16[2,112,128]{2,1,0:T(8,128)(2,1)S(1)}, u32[]{:S(2)}, u32[]{:S(2)}) %collective-permute-start.1) | collective-permute-done | bytes 57376 | tf_op jit(solution)/shard_map/ppermute | solution.py:202
  40.2 0.0 collective-permute-done.2
  40.2 2.0 %collective-permute-done.3 = bf16[2,112,128]{2,1,0:T(8,128)(2,1)S(1)} collective-permute-done((bf16[2,112,128]{2,1,0:T(8,128)(2,1)S(1)}, bf16[2,112,128]{2,1,0:T(8,128)(2,1)S(1)}, u32[]{:S(2)}, u32[]{:S(2)}) %collective-permute-start.3) | collective-permute-done | bytes 57376 | tf_op jit(solution)/shard_map/ppermute | solution.py:202
  42.2 7.6 %all-to-all-start.1 = ((bf16[32,56,128]{2,1,0:T(8,128)(2,1)}), bf16[32,56,128]{2,1,0:T(8,128)(2,1)S(1)}, u32[]{:S(2)}, u32[]{:S(2)}) async-start(bf16[32,56,128]{2,1,0:T(8,128)(2,1)} %bitcast), calls=%async_computation.1 | async-start | bytes 917504 | tf_op jit(solution)/shard_map/all_to_all | solution.py:210
  49.9 2.2 %collective-permute-start.4 = (bf16[2,112,128]{2,1,0:T(8,128)(2,1)S(1)}, bf16[2,112,128]{2,1,0:T(8,128)(2,1)S(1)}, u32[]{:S(2)}, u32[]{:S(2)}) collective-permute-start(bf16[2,112,128]{2,1,0:T(8,128)(2,1)S(1)} %add_add_fusion.mine_ref), channel_id=1, source_target_pairs={{0,1},{1,0},{2,3},{3,2},{4,5},{5,4},{6,7},{7,6},{8,9},{9,8},{10,11... | collective-permute-start | bytes 172040 | tf_op jit(solution)/shard_map/ppermute | solution.py:206
  52.0 5.2 %collective-permute-done.4.away_ref = bf16[2,112,128]{2,1,0:T(8,128)(2,1)S(1)} collective-permute-done((bf16[2,112,128]{2,1,0:T(8,128)(2,1)S(1)}, bf16[2,112,128]{2,1,0:T(8,128)(2,1)S(1)}, u32[]{:S(2)}, u32[]{:S(2)}) %collective-permute-start.4) | collective-permute-done | bytes 57376 | tf_op jit(solution)/shard_map/ppermute | solution.py:206
  57.2 3.6 %all-to-all-done.1.other_ref = bf16[32,56,128]{2,1,0:T(8,128)(2,1)S(1)} async-done(((bf16[32,56,128]{2,1,0:T(8,128)(2,1)}), bf16[32,56,128]{2,1,0:T(8,128)(2,1)S(1)}, u32[]{:S(2)}, u32[]{:S(2)}) %all-to-all-start.1) | async-done | bytes 458784 | tf_op jit(solution)/shard_map/all_to_all | solution.py:210
  60.8 1.8 %cross.1 = bf16[32,112,128]{2,1,0:T(8,128)(2,1)} custom-call(bf16[32,112,128]{2,1,0:T(8,128)(2,1)S(1)} %all-to-all-done.own_ref, bf16[32,56,128]{2,1,0:T(8,128)(2,1)S(1)} %all-to-all-done.1.other_ref, bf16[2,112,128]{2,1,0:T(8,128)(2,1)S(1)} %add_add_fusion.mine_ref, bf16[2,112,128]{2,1,0:T(8,128)(2,1)S(1)} %collective-permute-done.4.away_ref), custom_call_target="tpu_custom_call" | custom-call | tf_op jit(solution)/shard_map/cross/pallas_call | solution.py:150
  62.6 4.6 %all-to-all-start.2 = ((bf16[32,112,128]{2,1,0:T(8,128)(2,1)}), bf16[32,112,128]{2,1,0:T(8,128)(2,1)S(1)}, u32[]{:S(2)}, u32[]{:S(2)}) async-start(bf16[32,112,128]{2,1,0:T(8,128)(2,1)} %cross.1), calls=%async_computation.2 | async-start | bytes 1835008 | tf_op jit(solution)/shard_map/all_to_all | solution.py:210
  67.2 1.8 %cosine_convert_fusion = (bf16[1,200,400]{2,1,0:T(8,128)(2,1)S(1)}, bf16[1,200,400]{2,1,0:T(8,128)(2,1)S(1)}) fusion(s32[400]{0:T(512)S(1)} %iota_add_fusion), kind=kLoop, calls=%fused_computation.5 | loop fusion | flops 960000 | bytes 321600 | tf_op jit(solution)/shard_map/convert
  69.0 0.1 pad_maximum_fusion.refs_1_
  69.0 13.6 %all-to-all-done.2.refs_0_ = bf16[32,112,128]{2,1,0:T(8,128)(2,1)S(1)} async-done(((bf16[32,112,128]{2,1,0:T(8,128)(2,1)}), bf16[32,112,128]{2,1,0:T(8,128)(2,1)S(1)}, u32[]{:S(2)}, u32[]{:S(2)}) %all-to-all-start.2) | async-done | bytes 917536 | tf_op jit(solution)/shard_map/all_to_all | solution.py:210
  82.7 2.4 %lag.1 = bf16[2,16,32,400]{3,2,1,0:T(8,128)(2,1)} custom-call(bf16[32,112,128]{2,1,0:T(8,128)(2,1)S(1)} %all-to-all-done.2.refs_0_, bf16[2,200,400]{2,1,0:T(8,128)(2,1)S(1)} %pad_maximum_fusion.refs_1_), custom_call_target="tpu_custom_call" | custom-call | tf_op jit(solution)/shard_map/lag/pallas_call | solution.py:186
  (4 shorter events, 0.0 us)
Async XLA Ops:
  3.4 8.8 %copy-start.1 = (bf16[1600,128]{1,0:T(8,128)(2,1)S(1)}, bf16[1600,128]{1,0:T(8,128)(2,1)}, u32[]{:S(2)}) copy-start(bf16[1600,128]{1,0:T(8,128)(2,1)} %get-tuple-element.10) | copy-start | bytes 1228804
  3.4 24.3 %all-to-all-start = ((bf16[32,112,128]{2,1,0:T(8,128)(2,1)}), bf16[32,112,128]{2,1,0:T(8,128)(2,1)S(1)}, u32[]{:S(2)}, u32[]{:S(2)}) async-start(bf16[32,112,128]{2,1,0:T(8,128)(2,1)} %get-tuple-element.9), calls=%async_computation | async-start | bytes 1835008 | tf_op jit(solution)/shard_map/all_to_all | solution.py:210
  12.1 7.0 %copy-start = (s32[2]{0:T(128)S(1)}, s32[2]{0:T(128)}, u32[]{:S(2)}) copy-start(s32[2]{0:T(128)} %param.3) | copy-start | bytes 28
  12.2 20.3 %collective-permute-start = (bf16[1600,128]{1,0:T(8,128)(2,1)S(1)}, bf16[1600,128]{1,0:T(8,128)(2,1)S(1)}, u32[]{:S(2)}, u32[]{:S(2)}) collective-permute-start(bf16[1600,128]{1,0:T(8,128)(2,1)S(1)} %copy-done.1), channel_id=1, source_target_pairs={{0,1},{1,0},{2,3},{3,2},{4,5},{5,4},{6,7},{7,6},{8,9},{9,8},{10,11... | collective-permute-start | bytes 1228808 | tf_op jit(solution)/shard_map/ppermute | solution.py:206
  27.8 12.5 %collective-permute-start.1 = (bf16[2,112,128]{2,1,0:T(8,128)(2,1)S(1)}, bf16[2,112,128]{2,1,0:T(8,128)(2,1)S(1)}, u32[]{:S(2)}, u32[]{:S(2)}) collective-permute-start(bf16[2,112,128]{2,1,0:T(8,128)(2,1)S(1)} %pad_maximum_fusion.1), channel_id=1, source_target_pairs={{0,64},{64,0},{128,192},{192,128},{1,65},{65,1},{129,193},{193,129... | collective-permute-start | bytes 172040 | tf_op jit(solution)/shard_map/ppermute | solution.py:202
  29.5 10.7 %collective-permute-start.2 = (bf16[2,112,128]{2,1,0:T(8,128)(2,1)S(1)}, bf16[2,112,128]{2,1,0:T(8,128)(2,1)S(1)}, u32[]{:S(2)}, u32[]{:S(2)}) collective-permute-start(bf16[2,112,128]{2,1,0:T(8,128)(2,1)S(1)} %pad_maximum_fusion.1), channel_id=1, source_target_pairs={{0,128},{64,192},{128,0},{192,64},{1,129},{65,193},{129,1},{193,65... | collective-permute-start | bytes 172040 | tf_op jit(solution)/shard_map/ppermute | solution.py:202
  32.5 9.8 %collective-permute-start.3 = (bf16[2,112,128]{2,1,0:T(8,128)(2,1)S(1)}, bf16[2,112,128]{2,1,0:T(8,128)(2,1)S(1)}, u32[]{:S(2)}, u32[]{:S(2)}) collective-permute-start(bf16[2,112,128]{2,1,0:T(8,128)(2,1)S(1)} %pad_maximum_fusion.1), channel_id=1, source_target_pairs={{0,192},{64,128},{128,64},{192,0},{1,193},{65,129},{129,65},{193,1... | collective-permute-start | bytes 172040 | tf_op jit(solution)/shard_map/ppermute | solution.py:202
  42.2 18.6 %all-to-all-start.1 = ((bf16[32,56,128]{2,1,0:T(8,128)(2,1)}), bf16[32,56,128]{2,1,0:T(8,128)(2,1)S(1)}, u32[]{:S(2)}, u32[]{:S(2)}) async-start(bf16[32,56,128]{2,1,0:T(8,128)(2,1)} %bitcast), calls=%async_computation.1 | async-start | bytes 917504 | tf_op jit(solution)/shard_map/all_to_all | solution.py:210
  49.9 7.3 %collective-permute-start.4 = (bf16[2,112,128]{2,1,0:T(8,128)(2,1)S(1)}, bf16[2,112,128]{2,1,0:T(8,128)(2,1)S(1)}, u32[]{:S(2)}, u32[]{:S(2)}) collective-permute-start(bf16[2,112,128]{2,1,0:T(8,128)(2,1)S(1)} %add_add_fusion.mine_ref), channel_id=1, source_target_pairs={{0,1},{1,0},{2,3},{3,2},{4,5},{5,4},{6,7},{7,6},{8,9},{9,8},{10,11... | collective-permute-start | bytes 172040 | tf_op jit(solution)/shard_map/ppermute | solution.py:206
  62.6 20.1 %all-to-all-start.2 = ((bf16[32,112,128]{2,1,0:T(8,128)(2,1)}), bf16[32,112,128]{2,1,0:T(8,128)(2,1)S(1)}, u32[]{:S(2)}, u32[]{:S(2)}) async-start(bf16[32,112,128]{2,1,0:T(8,128)(2,1)} %cross.1), calls=%async_computation.2 | async-start | bytes 1835008 | tf_op jit(solution)/shard_map/all_to_all | solution.py:210
